TPU v7x, 32 devices: a whole 2x2x4 slice. The times are simulated.
32 devices in a mesh: gx: 4 (over z), gy: 2 (over core), ma: 4 (over y, x).
Axes of the slice: x: 2, y: 2, z: 4, core: 2. Of those that a mesh axis runs over, the one named last changes fastest.
Arguments:
- ensemble: float32 [80, 2, 16, 256], P('ma', None, 'gx', 'gy'), may hold values from -6 to 6
- wind_field: float32 [2, 2, 16, 256], P(None, None, 'gx', 'gy'), may hold values from -0.45 to 0.45
- obs_value: float32 [4, 1024], replicated, may hold values from -6 to 6
- obs_var: float32 [4, 1024], replicated, may hold values from 2 to 20
- obs_region: int32 [4, 1024], replicated, may hold values from 0 to 7, as said below
- obs_cell: int32 [4, 1024], replicated, may hold values from 0 to 1023
- block_order: int32 [4], replicated, may hold values from 0 to 3, each once
- localization: float32 [4, 2, 4, 1024], P('gx', 'gy'), may hold values from 0 to 1
Outputs:
- analysis: float32 [80, 2, 16, 256], P('ma', None, 'gx', 'gy')
Inputs may be any that keep to these rules, and one draw needn't show every extreme that they name: `obs_region`: region index = first-dimension region * 2 + second-dimension region.
All inputs are finite; a program needn't handle non-finite values.
Results may differ from a plain program's by a relative error of at most 0.0001.
Values sent between devices are 32-bit elements; how exact they have to be, the bound alone decides.
A program may use at most 64 MiB of HBM per device.

v0:
```python
import jax
import jax.numpy as jnp
from jax import lax
from jax.sharding import PartitionSpec as P

STEPS = 2
BLOCKS = 4


KAPPA = 0.025


def extended(block, sides, width):
    for axis, dim in sides:
        count = lax.axis_size(axis)
        forward = [(i, i + 1) for i in range(count - 1)]
        forward.append((count - 1, 0))
        backward = [(target, source) for source, target in forward]
        low = lax.ppermute(
            lax.slice_in_dim(block, block.shape[dim] - width, None, axis=dim), axis, forward
        )
        high = lax.ppermute(lax.slice_in_dim(block, 0, width, axis=dim), axis, backward)
        block = jnp.concatenate([low, block, high], axis=dim)
    return block


def advect(tracer, wind_field):
    padded = extended(tracer, (("gx", 2), ("gy", 3)), 1)
    east_wind = wind_field[0][None]
    north_wind = wind_field[1][None]
    middle = padded[:, :, 1:-1, 1:-1]
    west_side = padded[:, :, :-2, 1:-1]
    east_side = padded[:, :, 2:, 1:-1]
    south_side = padded[:, :, 1:-1, :-2]
    north_side = padded[:, :, 1:-1, 2:]
    return (
        middle
        - jnp.maximum(east_wind, 0.0) * (middle - west_side)
        - jnp.minimum(east_wind, 0.0) * (east_side - middle)
        - jnp.maximum(north_wind, 0.0) * (middle - south_side)
        - jnp.minimum(north_wind, 0.0) * (north_side - middle)
        + KAPPA * (east_side + west_side + north_side + south_side - 4.0 * middle)
    )


def mixing_matrix(prior_obs, observed, error_var, taper, ensemble_size):
    denom = ensemble_size - 1.0
    obs_mean = jnp.mean(prior_obs, axis=0)
    anomaly = prior_obs - obs_mean
    variance = jnp.sum(anomaly * anomaly, axis=0) / denom
    total_var = variance + error_var
    innovation = observed - obs_mean
    shrink = 1.0 / (1.0 + jnp.sqrt(error_var / total_var))
    gain_mean = taper * innovation / (denom * total_var)
    gain_spread = taper * shrink / (denom * total_var)
    shift_terms = jnp.dot(anomaly, gain_mean, precision=lax.Precision.HIGHEST)
    weighted = anomaly * gain_spread
    return shift_terms[:, None] - jnp.dot(weighted, anomaly.T, precision=lax.Precision.HIGHEST)


def local(
    ensemble, wind_field, obs_value, obs_var, obs_region, obs_cell, block_order, localization
):
    state = ensemble
    for step_index in range(STEPS):
        state = advect(state, wind_field)
    members_dev, levels, cells_x, cells_y = state.shape
    ensemble_size = members_dev * lax.axis_size("ma")
    own_region = lax.axis_index("gx") * lax.axis_size("gy") + lax.axis_index("gy")
    member_part = lax.axis_index("ma")
    stacked = state.reshape(members_dev, -1)
    for position in range(BLOCKS):
        block_id = block_order[position]
        gathered = lax.all_gather(stacked, "ma", axis=0, tiled=True)
        picked = jnp.take(gathered, obs_cell[block_id], axis=1)
        is_held = obs_region[block_id] == own_region
        prior_obs = lax.psum(jnp.where(is_held[None], picked, 0.0), ("gx", "gy"))
        mixing = mixing_matrix(
            prior_obs,
            obs_value[block_id],
            obs_var[block_id],
            localization[0, 0, block_id],
            ensemble_size,
        )
        center = jnp.mean(gathered, axis=0)
        own_columns = lax.dynamic_slice_in_dim(mixing, member_part * members_dev, members_dev, 1)
        stacked = stacked + jnp.dot(
            own_columns.T, gathered - center, precision=lax.Precision.HIGHEST
        )
    return stacked.reshape(state.shape)


def solution(mesh):
    in_specs = (
        P("ma", None, "gx", "gy"),
        P(None, None, "gx", "gy"),
        P(),
        P(),
        P(),
        P(),
        P(),
        P("gx", "gy", None, None),
    )
    out_specs = P("ma", None, "gx", "gy")
    return jax.shard_map(local, mesh=mesh, in_specs=in_specs, out_specs=out_specs, check_vma=False)
```

profile of v0, /device:TPU:0, one launch (start us, length us, event | category | flops | bytes accessed | tf_op | source)
XLA Modules:
  0.0 332.9 jit_solution(6084002492528208983)
XLA Ops:
  6.5 1.0 fusion.83
  7.6 5.1 %collective-permute-start.1 = (f32[20,2,1,128]{3,2,1,0:T(1,128)S(1)}, f32[20,2,1,128]{3,2,1,0:T(1,128)S(1)}, u32[]{:S(2)}, u32[]{:S(2)}) collective-permute-start(f32[20,2,1,128]{3,2,1,0:T(1,128)S(1)} %get-tuple-element.29), channel_id=1, source_target_pairs={{8,0},{16,8},{24,16},{0,24},{9,1},{17,9},{25,17},{1,25},{10,2},{18... | collective-permute-start | bytes 61448 | tf_op jit(solution)/shard_map/ppermute | solution.py:22
  12.7 0.7 fusion.84
  21.0 0.7 copy-done.10
  21.7 0.1 pad_maximum_fusion
  21.8 0.1 fusion.81
  21.9 0.1 collective-permute-start.3
  22.0 0.5 collective-permute-start.2
  22.5 0.9 collective-permute-done.3
  23.4 0.2 collective-permute-done.2
  23.6 0.4 fusion.56
  24.0 3.9 %collective-permute-start.5 = (f32[20,2,1,128]{3,2,1,0:T(1,128)S(1)}, f32[20,2,1,128]{3,2,1,0:T(1,128)S(1)}, u32[]{:S(2)}, u32[]{:S(2)}) collective-permute-start(f32[20,2,1,128]{3,2,1,0:T(1,128)S(1)} %get-tuple-element.27), channel_id=1, source_target_pairs={{8,0},{16,8},{24,16},{0,24},{9,1},{17,9},{25,17},{1,25},{10,2},{18... | collective-permute-start | bytes 61448 | tf_op jit(solution)/shard_map/ppermute | solution.py:22
  28.0 1.4 collective-permute-done.5
  29.4 4.1 %collective-permute-done.4 = f32[20,2,1,128]{3,2,1,0:T(1,128)S(1)} collective-permute-done((f32[20,2,1,128]{3,2,1,0:T(1,128)S(1)}, f32[20,2,1,128]{3,2,1,0:T(1,128)S(1)}, u32[]{:S(2)}, u32[]{:S(2)}) %collective-permute-start.4) | collective-permute-done | bytes 20512 | tf_op jit(solution)/shard_map/ppermute | solution.py:19
  33.6 0.1 fusion.80
  33.7 0.1 collective-permute-start.7
  33.8 0.5 collective-permute-start.6
  34.3 0.1 compare_reduce_fusion
  34.4 0.8 collective-permute-done.7
  35.1 0.2 collective-permute-done.6
  35.4 0.4 fusion.42
  35.8 9.5 %all-gather = f32[4,20,1024]{2,1,0:T(8,128)S(1)} all-gather(f32[1,20,1024]{2,1,0:T(8,128)S(1)} %reshape.117), channel_id=1, replica_groups=mesh['gx'=4,'gy'=2,'ma'=4] {'ma'}, dimensions={0}, use_global_device_ids=true | all-gather | bytes 409600 | tf_op jit(solution)/shard_map/all_gather | solution.py:74
  45.4 0.2 copy.17
  45.7 2.8 gather_fusion
  48.5 1.1 bitcast_select_fusion.3
  49.7 53.5 %all-reduce.5.cloned.1.call-done = f32[80,1024]{0,1:T(8,128)} async-done(((f32[80,1024]{0,1:T(8,128)}), f32[80,1024]{0,1:T(8,128)}) %all-reduce.5.cloned.1.call-update) | async-done | bytes 327696 | tf_op jit(solution)/shard_map/psum | solution.py:77
  103.2 1.3 reduce_sum.108
  104.5 0.4 multiply_reduce_fusion.3
  104.9 0.3 copy-done.5
  105.3 1.5 fusion.6
  106.8 0.5 convolution_bitcast_fusion.3
  107.3 0.3 convolution_add_fusion.3
  107.6 10.0 %all-gather.1 = f32[4,20,1024]{2,1,0:T(8,128)S(1)} all-gather(f32[1,20,1024]{2,1,0:T(8,128)S(1)} %bitcast.72), channel_id=1, replica_groups=mesh['gx'=4,'gy'=2,'ma'=4] {'ma'}, dimensions={0}, use_global_device_ids=true | all-gather | bytes 409600 | tf_op jit(solution)/shard_map/all_gather | solution.py:74
  117.7 0.2 copy.18
  117.9 2.8 gather_fusion.1
  120.7 1.1 bitcast_select_fusion.2
  121.9 54.3 %all-reduce.7.cloned.1.call-done = f32[80,1024]{0,1:T(8,128)} async-done(((f32[80,1024]{0,1:T(8,128)}), f32[80,1024]{0,1:T(8,128)}) %all-reduce.7.cloned.1.call-update) | async-done | bytes 327696 | tf_op jit(solution)/shard_map/psum | solution.py:77
  176.2 1.3 reduce_sum.111
  177.6 0.4 multiply_reduce_fusion.2
  178.0 1.5 fusion.4
  179.5 0.5 convolution_bitcast_fusion.2
  180.0 0.3 convolution_add_fusion.2
  180.3 10.0 %all-gather.2 = f32[4,20,1024]{2,1,0:T(8,128)S(1)} all-gather(f32[1,20,1024]{2,1,0:T(8,128)S(1)} %bitcast.73), channel_id=1, replica_groups=mesh['gx'=4,'gy'=2,'ma'=4] {'ma'}, dimensions={0}, use_global_device_ids=true | all-gather | bytes 409600 | tf_op jit(solution)/shard_map/all_gather | solution.py:74
  190.4 0.2 copy.19
  190.6 2.8 gather_fusion.2
  193.4 1.1 bitcast_select_fusion.1
  194.6 0.2 all-reduce.11.cloned.1.call-start
  194.8 54.1 %all-reduce.9.cloned.1.call-done = f32[80,1024]{0,1:T(8,128)} async-done(((f32[80,1024]{0,1:T(8,128)}), f32[80,1024]{0,1:T(8,128)}) %all-reduce.9.cloned.1.call-update) | async-done | bytes 327696 | tf_op jit(solution)/shard_map/psum | solution.py:77
  248.9 1.3 reduce_sum.114
  250.3 0.4 multiply_reduce_fusion.1
  250.7 1.5 fusion.2
  252.2 0.5 convolution_bitcast_fusion.1
  252.7 0.3 convolution_add_fusion.1
  253.0 10.0 %all-gather.3 = f32[4,20,1024]{2,1,0:T(8,128)S(1)} all-gather(f32[1,20,1024]{2,1,0:T(8,128)S(1)} %bitcast.71), channel_id=1, replica_groups=mesh['gx'=4,'gy'=2,'ma'=4] {'ma'}, dimensions={0}, use_global_device_ids=true | all-gather | bytes 409600 | tf_op jit(solution)/shard_map/all_gather | solution.py:74
  263.1 0.2 copy.20
  263.3 2.8 gather_fusion.3
  266.1 1.1 bitcast_select_fusion
  267.3 54.3 %all-reduce.11.cloned.1.call-done = f32[80,1024]{0,1:T(8,128)} async-done(((f32[80,1024]{0,1:T(8,128)}), f32[80,1024]{0,1:T(8,128)}) %all-reduce.11.cloned.1.call-update) | async-done | bytes 327696 | tf_op jit(solution)/shard_map/psum | solution.py:77
  321.6 1.3 reduce_sum.117
  323.0 0.4 multiply_reduce_fusion
  323.4 1.5 fusion
  324.9 0.5 convolution_bitcast_fusion
  325.4 0.3 convolution_add_fusion
  325.7 0.7 reshape.80
  (74 shorter events, 1.0 us)
Async XLA Ops:
  6.5 96.6 %all-reduce.5.cloned.1.call-start = ((), (), s32[]{:S(2)}) async-start(), calls=%async_computation | async-start | bytes 1048576 | tf_op jit(solution)/shard_map/psum | solution.py:77
  7.5 5.1 %copy-start.11 = (s32[4]{0:T(128)S(1)}, s32[4]{0:T(128)}, u32[]{:S(2)}) copy-start(s32[4]{0:T(128)} %param.16) | copy-start | bytes 52
  7.6 14.2 %collective-permute-start.1 = (f32[20,2,1,128]{3,2,1,0:T(1,128)S(1)}, f32[20,2,1,128]{3,2,1,0:T(1,128)S(1)}, u32[]{:S(2)}, u32[]{:S(2)}) collective-permute-start(f32[20,2,1,128]{3,2,1,0:T(1,128)S(1)} %get-tuple-element.29), channel_id=1, source_target_pairs={{8,0},{16,8},{24,16},{0,24},{9,1},{17,9},{25,17},{1,25},{10,2},{18... | collective-permute-start | bytes 61448 | tf_op jit(solution)/shard_map/ppermute | solution.py:22
  12.7 8.3 %copy-start.7 = (s32[4,1024]{1,0:T(4,128)S(1)}, s32[4,1024]{1,0:T(4,128)}, u32[]{:S(2)}) copy-start(s32[4,1024]{1,0:T(4,128)} %param.15) | copy-start | bytes 49156
  12.7 9.1 %copy-start.4 = (f32[20,2,4,128]{3,2,1,0:T(4,128)S(1)}, f32[20,2,4,128]{3,2,1,0:T(4,128)}, u32[]{:S(2)}) copy-start(f32[20,2,4,128]{3,2,1,0:T(4,128)} %param.10) | copy-start | bytes 245764
  12.7 9.1 %collective-permute-start = (f32[20,2,1,128]{3,2,1,0:T(1,128)S(1)}, f32[20,2,1,128]{3,2,1,0:T(1,128)S(1)}, u32[]{:S(2)}, u32[]{:S(2)}) collective-permute-start(f32[20,2,1,128]{3,2,1,0:T(1,128)S(1)} %get-tuple-element.28), channel_id=1, source_target_pairs={{0,8},{8,16},{16,24},{24,0},{1,9},{9,17},{17,25},{25,1},{2,10},{10... | collective-permute-start | bytes 61448 | tf_op jit(solution)/shard_map/ppermute | solution.py:19
  21.0 0.7 copy-start.10
  21.9 1.5 collective-permute-start.3
  22.0 1.6 collective-permute-start.2
  24.0 3.9 %copy-start.8 = (f32[4,1024]{1,0:T(4,128)S(1)}, f32[4,1024]{1,0:T(4,128)}, u32[]{:S(2)}) copy-start(f32[4,1024]{1,0:T(4,128)} %param.12) | copy-start | bytes 49156
  24.0 5.4 %collective-permute-start.5 = (f32[20,2,1,128]{3,2,1,0:T(1,128)S(1)}, f32[20,2,1,128]{3,2,1,0:T(1,128)S(1)}, u32[]{:S(2)}, u32[]{:S(2)}) collective-permute-start(f32[20,2,1,128]{3,2,1,0:T(1,128)S(1)} %get-tuple-element.27), channel_id=1, source_target_pairs={{8,0},{16,8},{24,16},{0,24},{9,1},{17,9},{25,17},{1,25},{10,2},{18... | collective-permute-start | bytes 61448 | tf_op jit(solution)/shard_map/ppermute | solution.py:22
  27.9 5.6 %collective-permute-start.4 = (f32[20,2,1,128]{3,2,1,0:T(1,128)S(1)}, f32[20,2,1,128]{3,2,1,0:T(1,128)S(1)}, u32[]{:S(2)}, u32[]{:S(2)}) collective-permute-start(f32[20,2,1,128]{3,2,1,0:T(1,128)S(1)} %get-tuple-element.26), channel_id=1, source_target_pairs={{0,8},{8,16},{16,24},{24,0},{1,9},{9,17},{17,25},{25,1},{2,10},{10... | collective-permute-start | bytes 61448 | tf_op jit(solution)/shard_map/ppermute | solution.py:19
  33.6 0.7 copy-start.9
  33.7 1.5 collective-permute-start.7
  33.8 1.6 collective-permute-start.6
  49.6 126.6 %all-reduce.7.cloned.1.call-start = ((), (), s32[]{:S(2)}) async-start(), calls=%async_computation.1 | async-start | bytes 1048576 | tf_op jit(solution)/shard_map/psum | solution.py:77
  103.2 1.3 copy-start
  104.5 0.7 copy-start.5
  104.5 0.7 copy-start.6
  121.9 127.0 %all-reduce.9.cloned.1.call-start = ((), (), s32[]{:S(2)}) async-start(), calls=%async_computation.2 | async-start | bytes 1048576 | tf_op jit(solution)/shard_map/psum | solution.py:77
  176.2 1.3 copy-start.1
  194.6 127.0 %all-reduce.11.cloned.1.call-start = ((), (), s32[]{:S(2)}) async-start(), calls=%async_computation.3 | async-start | bytes 1048576 | tf_op jit(solution)/shard_map/psum | solution.py:77
  248.9 1.3 copy-start.2
  321.6 1.3 copy-start.3
Sparse Core Ops, SparseCore 0:
  49.8 53.3 all-reduce.4
  122.0 54.1 all-reduce.6
  194.7 54.1 all-reduce.8
  267.4 54.1 all-reduce.10
where the time goes:
time: 334 us; the launch traced here: 333 us
  waiting for transfers between devices  224 us (67%)
  blocking collectives  39.5 us (12%)
  between operations  21.3 us (6%)
  local copies, waits for them, and re-layouts  15.9 us (5%)
  other arithmetic  12.7 us (4%)
  starting transfers between devices  10.4 us (3%)
  matrix products  9.05 us (3%)
    psum x4, waiting for transfers between devices, local(): prior_obs = lax.psum(jnp.where(is_held[None], picked, 0.0), ('gx', 'gy'))  216 us
    all_gather x4, blocking collectives, local(): gathered = lax.all_gather(stacked, 'ma', axis=0, tiled=True)  39.5 us
    gather x4, local copies, waits for them, and re-layouts, local(): picked = jnp.take(gathered, obs_cell[block_id], axis=1)  11.2 us
    ppermute x4, starting transfers between devices, extended(): lax.ppermute(lax.slice_in_dim(block, 0, width, axis=dim), axis, backward)  9.11 us
  transfers between devices with their start and end apart: 12, of which 10 were waited for; matrix products, arithmetic and copies ran while one was open for 0% of the time, Pallas kernels for 0%

commit v1 on v0

v1 whole, which is shorter than its diff:
```python
import functools

import jax
import jax.numpy as jnp
from jax import lax
from jax.experimental import pallas as pl
from jax.experimental.pallas import tpu as pltpu
from jax.sharding import PartitionSpec as P

STEPS = 2
KAPPA = 0.025
PAD = 128
MESH = pl.DeviceIdType.MESH
BF = jnp.bfloat16
F32 = jnp.float32


def split(x):
    high = x.astype(BF)
    return high, (x - high.astype(F32)).astype(BF)


def kernel(
    nx, ny, nm,
    order_ref, ens_ref, wind_ref, value_ref, var_ref, region_ref, cell_ref, loc_ref,
    out_ref,
    o_ens, o_wind, up_ref, down_ref, low_ref, high_ref, ext_ref, piece_ref,
    all_ref, split_ref, loc_all, hot_ref, prior_ref, lhs_ref, gm_ref, anom_ref,
    send_ref, pair_ref, line_ref, full_ref,
    pre_sem, halo_sem, loc_send, loc_recv, plane_send, plane_recv,
    pair_sem, line_send, line_recv,
):
    members_dev, levels, cx, cy = ens_ref.shape
    half = members_dev // 2
    members = members_dev * nm
    blocks, obs = value_ref.shape
    cells = levels * cx * cy
    gx, gy, ma = lax.axis_index("gx"), lax.axis_index("gy"), lax.axis_index("ma")
    other = 1 - gy

    def remote(src, dst, send_sem, recv_sem, device):
        return pltpu.make_async_remote_copy(
            src_ref=src, dst_ref=dst, send_sem=send_sem, recv_sem=recv_sem,
            device_id=device, device_id_type=MESH,
        )

    line = [(lax.rem(gx + d, nx), c) for d in range(nx) for c in range(ny) if d or c]
    line = [(x, lax.rem(gy + c, ny)) for x, c in line]
    plane = [(lax.rem(ma + d, nm), lax.rem(gy + c, ny)) for d in range(nm) for c in range(ny) if d or c]

    barrier = pltpu.get_barrier_semaphore()
    for x, c in line:
        pl.semaphore_signal(barrier, inc=1, device_id=(x, c, ma), device_id_type=MESH)
    for m, c in plane[ny - 1:]:
        pl.semaphore_signal(barrier, inc=1, device_id=(gx, c, m), device_id_type=MESH)
    pl.semaphore_wait(barrier, len(line) + len(plane) - (ny - 1))

    swap = [
        remote(ens_ref.at[pl.ds(other * half, half)], o_ens, pre_sem.at[0], pre_sem.at[1], (gx, other, ma)),
        remote(wind_ref, o_wind, pre_sem.at[2], pre_sem.at[3], (gx, other, ma)),
    ]
    for copy in swap:
        copy.start()

    split_ref[...] = jnp.zeros_like(split_ref)
    anom_ref[...] = jnp.zeros_like(anom_ref)
    prior_ref[...] = jnp.zeros_like(prior_ref)

    for copy in swap:
        copy.wait()

    left = gy == 0
    own_t = ens_ref[pl.ds(gy * half, half)]
    for lev in range(levels):
        pairs = (
            (own_t[:, lev], o_ens[:, lev], slice(0, half)),
            (wind_ref[:, lev], o_wind[:, lev], slice(half, half + 2)),
        )
        for mine, theirs, where in pairs:
            first = jnp.where(left, mine, theirs)
            second = jnp.where(left, theirs, mine)
            for part, lanes in ((first, slice(0, cy)), (second, slice(cy, 2 * cy))):
                ext_ref[where, lev, 2:2 + cx, lanes] = part
                up_ref[where, 2 * lev:2 * lev + 2, lanes] = part[:, cx - 2:cx]
                down_ref[where, 2 * lev:2 * lev + 2, lanes] = part[:, 0:2]
    after, before = lax.rem(gx + 1, nx), lax.rem(gx + nx - 1, nx)
    halo = [
        remote(up_ref, low_ref, halo_sem.at[0], halo_sem.at[1], (after, gy, ma)),
        remote(down_ref, high_ref, halo_sem.at[2], halo_sem.at[3], (before, gy, ma)),
    ]
    for copy in halo:
        copy.start()

    own_region = gx * ny + gy
    loc_copies = []
    for i, (x, c) in enumerate(line):
        source = x * ny + c
        copy = remote(loc_ref.at[0, 0], loc_all.at[own_region], loc_send.at[i], loc_recv.at[own_region], (x, c, ma))
        copy.start()
        loc_copies.append((copy, remote(loc_ref.at[0, 0], loc_all.at[source], loc_send.at[i], loc_recv.at[source], (x, c, ma))))
    loc_all[own_region] = loc_ref[0, 0]

    def make_hot(k):
        b = order_ref[k]
        cell = jnp.where(region_ref[pl.ds(b, 1), :] == own_region, cell_ref[pl.ds(b, 1), :], -1)
        for s in range(cells // PAD):
            index = lax.broadcasted_iota(jnp.int32, (PAD, obs), 0) + s * PAD
            hot_ref[s * PAD:(s + 1) * PAD, :] = jnp.where(index == cell, 1.0, 0.0).astype(BF)

    make_hot(0)
    for copy in halo:
        copy.wait()

    for lev in range(levels):
        ext_ref[:, lev, 0:2, :] = low_ref[:, 2 * lev:2 * lev + 2, :]
        ext_ref[:, lev, 2 + cx:4 + cx, :] = high_ref[:, 2 * lev:2 * lev + 2, :]
    for lev in range(levels):
        east_wind = ext_ref[half, lev][None]
        north_wind = ext_ref[half + 1, lev][None]
        q = ext_ref[0:half, lev]
        for _ in range(STEPS):
            west = pltpu.roll(q, 1, 1)
            east = pltpu.roll(q, cx + 3, 1)
            south = pltpu.roll(q, 1, 2)
            north = pltpu.roll(q, 2 * cy - 1, 2)
            q = (
                q
                - jnp.maximum(east_wind, 0.0) * (q - west)
                - jnp.minimum(east_wind, 0.0) * (east - q)
                - jnp.maximum(north_wind, 0.0) * (q - south)
                - jnp.minimum(north_wind, 0.0) * (north - q)
                + KAPPA * (east + west + north + south - 4.0 * q)
            )
        for c in range(ny):
            piece_ref[c, :, lev * cx:(lev + 1) * cx, :] = q[:, 2:2 + cx, c * cy:(c + 1) * cy]

    own_part = ma * ny + gy
    plane_copies = []
    for i, (m, c) in enumerate(plane):
        source = m * ny + c
        copy = remote(
            piece_ref.at[c], all_ref.at[pl.ds(own_part * half, half)],
            plane_send.at[i], plane_recv.at[own_part], (gx, c, m),
        )
        copy.start()
        plane_copies.append((copy, remote(
            piece_ref.at[gy], all_ref.at[pl.ds(source * half, half)],
            plane_send.at[i], plane_recv.at[source], (gx, c, m),
        )))
    all_ref[pl.ds(own_part * half, half)] = piece_ref[gy]
    for sent, received in plane_copies:
        sent.wait_send()
        received.wait_recv()

    rows = levels * cx
    for s in range(rows):
        high, low = split(all_ref[:, s, :])
        split_ref[0, 0:members, s * cy:(s + 1) * cy] = high
        split_ref[1, 0:members, s * cy:(s + 1) * cy] = low

    def pick():
        for part in range(2):
            prior_ref[part, 0:members, :] = jnp.dot(
                split_ref[part, 0:members, :], hot_ref[...], preferred_element_type=F32
            ).astype(BF)

    pick()
    for sent, received in loc_copies:
        sent.wait_send()
        received.wait_recv()

    def apply(change, high, low):
        c_high, c_low = split(change)
        both = jnp.dot(jnp.concatenate([c_high, c_low], axis=0), high, preferred_element_type=F32)
        rest = jnp.dot(c_high, low, preferred_element_type=F32)
        return both[:members] + both[members:] + rest

    width = 4 if nx % 4 == 0 else nx
    in_group = width * ny
    lane = lax.broadcasted_iota(jnp.int32, (members, PAD), 1)
    change = None
    denom = members - 1.0
    for k in range(blocks):
        slot = k % 2
        b = order_ref[k]
        prior = prior_ref[0, 0:members, :].astype(F32) + prior_ref[1, 0:members, :].astype(F32)
        if k:
            prior = prior + apply(change, prior_ref[0], prior_ref[1])
        error_var = var_ref[pl.ds(b, 1), :]
        obs_mean = jnp.sum(prior, axis=0, keepdims=True) / members
        anomaly = prior - obs_mean
        variance = jnp.sum(anomaly * anomaly, axis=0, keepdims=True) / denom
        total_var = variance + error_var
        innovation = value_ref[pl.ds(b, 1), :] - obs_mean
        shrink = 1.0 / (1.0 + jnp.sqrt(error_var / total_var))
        scaled = 1.0 / (denom * total_var)
        mean_gain = innovation * scaled
        spread_gain = shrink * scaled
        a_high, a_low = split(anomaly)
        anom_ref[0:members, :] = a_high
        anom_ref[PAD:PAD + members, :] = a_low

        def group(g):
            for j in range(width):
                for c in range(ny):
                    i = j * ny + c
                    taper = loc_all[(g * width + j) * ny + c, pl.ds(b, 1), :]
                    w_high, w_low = split(anomaly * (taper * spread_gain))
                    lhs_ref[2 * i * members:(2 * i + 1) * members, :] = w_high
                    lhs_ref[(2 * i + 1) * members:(2 * i + 2) * members, :] = w_low
                    gm_ref[i:i + 1, :] = taper * mean_gain
            end = 2 * in_group * members
            g_high, g_low = split(gm_ref[...])
            lhs_ref[end:end + 16, :] = jnp.concatenate([g_high, g_low], axis=0)
            product = lax.dot_general(
                lhs_ref[...], anom_ref[...], (((1,), (1,)), ((), ())), preferred_element_type=F32
            )
            shift = product[end:end + 8, :PAD] + product[end:end + 8, PAD:] + product[end + 8:end + 16, :PAD]
            for j in range(width):
                for c in range(ny):
                    i = j * ny + c
                    first = product[2 * i * members:(2 * i + 1) * members]
                    second = product[(2 * i + 1) * members:(2 * i + 2) * members, :PAD]
                    spread = first[:, :PAD] + first[:, PAD:] + second
                    send_ref[slot, c, g * width + j] = shift[i:i + 1] - spread

        if nx == width:
            group(0)
        else:
            lax.fori_loop(0, nx // width, lambda g, carry: (group(g), carry)[1], 0)

        pair = remote(
            send_ref.at[slot, other], pair_ref.at[slot], pair_sem.at[slot, 0], pair_sem.at[slot, 1], (gx, other, ma)
        )
        pair.start()
        pair.wait()
        copies = []
        for d in range(nx):
            x = lax.rem(gx + d, nx)
            send_ref[slot, gy, x] = send_ref[slot, gy, x] + pair_ref[slot, x]
            if d:
                copy = remote(
                    send_ref.at[slot, gy, x], line_ref.at[slot, gx],
                    line_send.at[slot, d], line_recv.at[slot, gx], (x, gy, ma),
                )
                copy.start()
                copies.append((copy, remote(
                    send_ref.at[slot, gy, x], line_ref.at[slot, x],
                    line_send.at[slot, d], line_recv.at[slot, x], (x, gy, ma),
                )))
            else:
                line_ref[slot, gx] = send_ref[slot, gy, x]
        if k + 1 < blocks:
            make_hot(k + 1)
            pick()
        for sent, received in copies:
            sent.wait_send()
            received.wait_recv()
        mixing = line_ref[slot, 0]
        for x in range(1, nx):
            mixing = mixing + line_ref[slot, x]
        centre = jnp.sum(mixing, axis=1, keepdims=True) / members
        mixing = jnp.where(lane < members, mixing - centre, 0.0)
        if k:
            padded = jnp.concatenate([change, jnp.zeros((PAD - members, PAD), F32)], axis=0)
            change = change + mixing + jnp.dot(
                mixing, padded, precision=lax.Precision.HIGHEST, preferred_element_type=F32
            )
        else:
            change = mixing

    update = apply(change, split_ref[0], split_ref[1])
    for s in range(rows):
        full_ref[:, s, :] = all_ref[:, s, :] + update[:, s * cy:(s + 1) * cy]
    mine = full_ref[pl.ds(ma * members_dev, members_dev)]
    for lev in range(levels):
        out_ref[:, lev] = mine[:, lev * cx:(lev + 1) * cx, :]


def local(
    ensemble, wind_field, obs_value, obs_var, obs_region, obs_cell, block_order, localization
):
    nx, ny, nm = lax.axis_size("gx"), lax.axis_size("gy"), lax.axis_size("ma")
    members_dev, levels, cx, cy = ensemble.shape
    half = members_dev // 2
    members = members_dev * nm
    blocks, obs = obs_value.shape
    rows = levels * cx
    cells = rows * cy
    regions = nx * ny
    width = 4 if nx % 4 == 0 else nx
    in_group = width * ny
    dma = pltpu.SemaphoreType.DMA
    vmem = pl.BlockSpec(memory_space=pltpu.VMEM)
    return pl.pallas_call(
        functools.partial(kernel, nx, ny, nm),
        out_shape=jax.ShapeDtypeStruct(ensemble.shape, F32),
        in_specs=[pl.BlockSpec(memory_space=pltpu.SMEM)] + [vmem] * 7,
        out_specs=vmem,
        scratch_shapes=[
            pltpu.VMEM((half, levels, cx, cy), F32),
            pltpu.VMEM(wind_field.shape, F32),
            pltpu.VMEM((half + 2, 2 * levels, 2 * cy), F32),
            pltpu.VMEM((half + 2, 2 * levels, 2 * cy), F32),
            pltpu.VMEM((half + 2, 2 * levels, 2 * cy), F32),
            pltpu.VMEM((half + 2, 2 * levels, 2 * cy), F32),
            pltpu.VMEM((half + 2, levels, cx + 4, 2 * cy), F32),
            pltpu.VMEM((ny, half, rows, cy), F32),
            pltpu.VMEM((members, rows, cy), F32),
            pltpu.VMEM((2, PAD, cells), BF),
            pltpu.VMEM((regions, blocks, obs), F32),
            pltpu.VMEM((cells, obs), BF),
            pltpu.VMEM((2, PAD, obs), BF),
            pltpu.VMEM((2 * in_group * members + 16, obs), BF),
            pltpu.VMEM((8, obs), F32),
            pltpu.VMEM((2 * PAD, obs), BF),
            pltpu.VMEM((2, ny, nx, members, PAD), F32),
            pltpu.VMEM((2, nx, members, PAD), F32),
            pltpu.VMEM((2, nx, members, PAD), F32),
            pltpu.VMEM((members, rows, cy), F32),
            dma((4,)),
            dma((4,)),
            dma((regions,)),
            dma((regions,)),
            dma((nm * ny,)),
            dma((nm * ny,)),
            dma((2, 2)),
            dma((2, nx)),
            dma((2, nx)),
        ],
        compiler_params=pltpu.CompilerParams(
            collective_id=0, has_side_effects=True, vmem_limit_bytes=56 * 1024 * 1024
        ),
    )(block_order, ensemble, wind_field, obs_value, obs_var, obs_region, obs_cell, localization)


def solution(mesh):
    in_specs = (
        P("ma", None, "gx", "gy"),
        P(None, None, "gx", "gy"),
        P(),
        P(),
        P(),
        P(),
        P(),
        P("gx", "gy", None, None),
    )
    out_specs = P("ma", None, "gx", "gy")
    return jax.shard_map(local, mesh=mesh, in_specs=in_specs, out_specs=out_specs, check_vma=False)
```

time: 334 us -> 56.3 us (0.17)
  waiting for transfers between devices: 224 us -> 0 us
  Pallas kernels: 0 us -> 54.6 us
  blocking collectives: 39.5 us -> 0 us
  between operations: 21.3 us -> 0.01 us
  local copies, waits for them, and re-layouts: 15.9 us -> 1.53 us
  other arithmetic: 12.7 us -> 0 us
  starting transfers between devices: 10.4 us -> 0 us
  matrix products: 9.05 us -> 0 us
    psum x4 -> x0, waiting for transfers between devices: 216 us -> none  [local(): prior_obs = lax.psum(jnp.where(is_held[None], picked, 0.0), ('gx', 'gy'))]
    pallas_call x0 -> x1, Pallas kernels: none -> 54.6 us  [local(): pl.pallas_call(functools.partial(kernel, nx, ny, nm), out_shape=jax.Shape...]
    all_gather x4 -> x0, blocking collectives: 39.5 us -> none  [local(): gathered = lax.all_gather(stacked, 'ma', axis=0, tiled=True)]
    gather x4 -> x0, local copies, waits for them, and re-layouts: 11.2 us -> none  [local(): picked = jnp.take(gathered, obs_cell[block_id], axis=1)]
    ppermute x8 -> x0, starting transfers between devices: 10.1 us -> none  [the longest x4 9.11 us: extended(): lax.ppermute(lax.slice_in_dim(block, 0, width, axis=dim), axis, backward)]
    dot_general x12 -> x0, matrix products: 9.05 us -> none  [the longest x4 5.88 us: mixing_matrix(): jnp.dot(weighted, anomaly.T, precision=lax.Precision.HIGHEST)]
    ppermute x8 -> x0, waiting for transfers between devices: 7.68 us -> none  [the longest x4 4.57 us: extended(): lax.ppermute(lax.slice_in_dim(block, block.shape[dim] - width, None, axis...]
    reduce_sum x12 -> x0, other arithmetic: 6.85 us -> none  [the longest x4 5.26 us: mixing_matrix(): obs_mean = jnp.mean(prior_obs, axis=0)]
  transfers between devices with their start and end apart: 12 -> 0, of which waited for: 10 -> 0; matrix products, arithmetic and copies ran while one was open for 0% -> 0% of each run, Pallas kernels for 0% -> 0%
where the time goes in v1:
time: 56.3 us; the launch traced here: 56.1 us
  Pallas kernels  54.6 us (97%)
  local copies, waits for them, and re-layouts  1.53 us (3%)
    pallas_call x1, Pallas kernels, local(): pl.pallas_call(functools.partial(kernel, nx, ny, nm), out_shape=jax.Shape...  54.6 us
    unnamed x1, local copies, waits for them, and re-layouts  1.53 us

profile of v1, /device:TPU:0, one launch (start us, length us, event | category | flops | bytes accessed | tf_op | source)
XLA Modules:
  0.0 56.1 jit_solution(2720504729036781585)
XLA Ops:
  0.0 54.6 %shard_map.82 = f32[20,2,4,128]{3,2,1,0:T(4,128)} custom-call(s32[4]{0:T(128)} %order_ref.1, f32[20,2,4,128]{3,2,1,0:T(4,128)} %ens_ref.1, f32[2,2,4,128]{3,2,1,0:T(4,128)} %wind_ref.1, f32[4,1024]{1,0:T(4,128)} %value_ref.1, f32[4,1024]{1,0:T(4,128)} %var_ref.1, s32[4,1024]{1,0:T(4,128)} %region_ref.1, s32[4,1024]{1,0:T(4,128)} %cell_ref.1, ...), custom_call_target="tpu_custom_call" | custom-call | tf_op jit(solution)/shard_map/pallas_call | solution.py:295
  54.6 1.5 %copy.10 = f32[20,2,4,128]{3,2,1,0:T(4,128)} copy(f32[20,2,4,128]{3,2,1,0:T(4,128)} %shard_map.82) | data formatting | bytes 163840

commit v2 on v1

v2 whole, which is shorter than its diff:
```python
import functools

import jax
import jax.numpy as jnp
from jax import lax
from jax.experimental import pallas as pl
from jax.experimental.pallas import tpu as pltpu
from jax.sharding import PartitionSpec as P

STEPS = 2
KAPPA = 0.025
PAD = 128
MESH = pl.DeviceIdType.MESH
BF = jnp.bfloat16
F32 = jnp.float32


def split(x):
    high = x.astype(BF)
    return high, (x - high.astype(F32)).astype(BF)


def kernel(
    nx, ny, nm,
    order_ref, ens_ref, wind_ref, value_ref, var_ref, region_ref, cell_ref, loc_ref,
    out_ref,
    o_ens, o_wind, up_ref, down_ref, low_ref, high_ref, ext_ref, piece_ref,
    all_ref, flat_ref, split_ref, loc_all, hot_ref, lhs_ref, gm_ref, anom_ref,
    send_ref, pair_ref, line_ref,
    swap_sem, halo_send, halo_recv, loc_send, loc_recv, plane_send, plane_recv,
    pair_sem, line_send, line_recv,
):
    members_dev, levels, cx, cy = ens_ref.shape
    half = members_dev // 2
    members = members_dev * nm
    mid = members // 2
    blocks, obs = value_ref.shape
    cells = levels * cx * cy
    rows = levels * cx
    gx, gy, ma = lax.axis_index("gx"), lax.axis_index("gy"), lax.axis_index("ma")
    other = 1 - gy

    def remote(src, dst, send_sem, recv_sem, device):
        return pltpu.make_async_remote_copy(
            src_ref=src, dst_ref=dst, send_sem=send_sem, recv_sem=recv_sem,
            device_id=device, device_id_type=MESH,
        )

    line = [(lax.rem(gx + d, nx), c) for d in range(nx) for c in range(ny) if d or c]
    line = [(x, lax.rem(gy + c, ny)) for x, c in line]
    plane = [(lax.rem(ma + d, nm), lax.rem(gy + c, ny)) for d in range(nm) for c in range(ny) if d or c]

    barrier = pltpu.get_barrier_semaphore()
    for x, c in line:
        pl.semaphore_signal(barrier, inc=1, device_id=(x, c, ma), device_id_type=MESH)
    for m, c in plane[ny - 1:]:
        pl.semaphore_signal(barrier, inc=1, device_id=(gx, c, m), device_id_type=MESH)

    for c in range(ny):
        for lev in range(levels):
            pair_rows = slice(2 * lev, 2 * lev + 2)
            part = ens_ref[c * half:(c + 1) * half, lev]
            winds = wind_ref[:, lev]
            up_ref[c, 0:half, pair_rows, :] = part[:, cx - 2:cx]
            up_ref[c, half:half + 2, pair_rows, :] = winds[:, cx - 2:cx]
            down_ref[c, 0:half, pair_rows, :] = part[:, 0:2]
            down_ref[c, half:half + 2, pair_rows, :] = winds[:, 0:2]
    anom_ref[...] = jnp.zeros_like(anom_ref)
    gm_ref[...] = jnp.zeros_like(gm_ref)

    pl.semaphore_wait(barrier, len(line) + len(plane) - (ny - 1))

    after, before = lax.rem(gx + 1, nx), lax.rem(gx + nx - 1, nx)
    halo = []
    for c in range(ny):
        for way, (src, dst, to, source) in enumerate(
            ((up_ref, low_ref, after, before), (down_ref, high_ref, before, after))
        ):
            copy = remote(src.at[c], dst.at[gy], halo_send.at[way, c], halo_recv.at[way, gy], (to, c, ma))
            copy.start()
            halo.append((copy, remote(
                src.at[c], dst.at[c], halo_send.at[way, c], halo_recv.at[way, c], (source, c, ma)
            )))
    swap = [
        remote(ens_ref.at[pl.ds(other * half, half)], o_ens, swap_sem.at[0], swap_sem.at[1], (gx, other, ma)),
        remote(wind_ref, o_wind, swap_sem.at[2], swap_sem.at[3], (gx, other, ma)),
    ]
    for copy in swap:
        copy.start()

    own_region = gx * ny + gy
    loc_copies = []
    for i, (x, c) in enumerate(line):
        source = x * ny + c
        copy = remote(loc_ref.at[0, 0], loc_all.at[own_region], loc_send.at[i], loc_recv.at[own_region], (x, c, ma))
        copy.start()
        loc_copies.append((copy, remote(loc_ref.at[0, 0], loc_all.at[source], loc_send.at[i], loc_recv.at[source], (x, c, ma))))
    loc_all[own_region] = loc_ref[0, 0]

    def make_hot(k):
        b = order_ref[k]
        cell = jnp.where(region_ref[pl.ds(b, 1), :] == own_region, cell_ref[pl.ds(b, 1), :], -1)
        for s in range(cells // PAD):
            index = lax.broadcasted_iota(jnp.int32, (PAD, obs), 0) + s * PAD
            hot_ref[s * PAD:(s + 1) * PAD, :] = jnp.where(index == cell, 1.0, 0.0).astype(BF)

    make_hot(0)
    for copy in swap:
        copy.wait()

    left = gy == 0
    own_t = ens_ref[pl.ds(gy * half, half)]
    for lev in range(levels):
        pairs = (
            (own_t[:, lev], o_ens[:, lev], slice(0, half)),
            (wind_ref[:, lev], o_wind[:, lev], slice(half, half + 2)),
        )
        for mine, theirs, where in pairs:
            ext_ref[where, lev, 2:2 + cx, 0:cy] = jnp.where(left, mine, theirs)
            ext_ref[where, lev, 2:2 + cx, cy:2 * cy] = jnp.where(left, theirs, mine)
    for sent, received in halo:
        sent.wait_send()
        received.wait_recv()

    for lev in range(levels):
        for c in range(ny):
            lanes = slice(c * cy, (c + 1) * cy)
            ext_ref[:, lev, 0:2, lanes] = low_ref[c, :, 2 * lev:2 * lev + 2, :]
            ext_ref[:, lev, 2 + cx:4 + cx, lanes] = high_ref[c, :, 2 * lev:2 * lev + 2, :]
    for lev in range(levels):
        east_wind = ext_ref[half, lev][None]
        north_wind = ext_ref[half + 1, lev][None]
        q = ext_ref[0:half, lev]
        for _ in range(STEPS):
            west = pltpu.roll(q, 1, 1)
            east = pltpu.roll(q, cx + 3, 1)
            south = pltpu.roll(q, 1, 2)
            north = pltpu.roll(q, 2 * cy - 1, 2)
            q = (
                q
                - jnp.maximum(east_wind, 0.0) * (q - west)
                - jnp.minimum(east_wind, 0.0) * (east - q)
                - jnp.maximum(north_wind, 0.0) * (q - south)
                - jnp.minimum(north_wind, 0.0) * (north - q)
                + KAPPA * (east + west + north + south - 4.0 * q)
            )
        for c in range(ny):
            piece_ref[c, :, lev * cx:(lev + 1) * cx, :] = q[:, 2:2 + cx, c * cy:(c + 1) * cy]

    own_part = ma * ny + gy
    plane_copies = []
    for i, (m, c) in enumerate(plane):
        source = m * ny + c
        copy = remote(
            piece_ref.at[c], all_ref.at[pl.ds(own_part * half, half)],
            plane_send.at[i], plane_recv.at[own_part], (gx, c, m),
        )
        copy.start()
        plane_copies.append((copy, remote(
            piece_ref.at[gy], all_ref.at[pl.ds(source * half, half)],
            plane_send.at[i], plane_recv.at[source], (gx, c, m),
        )))
    all_ref[pl.ds(own_part * half, half)] = piece_ref[gy]
    for sent, received in plane_copies:
        sent.wait_send()
        received.wait_recv()

    for s in range(rows):
        lanes = slice(s * cy, (s + 1) * cy)
        values = all_ref[:, s, :]
        flat_ref[:, lanes] = values
        high, low = split(values)
        split_ref[0:members, lanes] = high
        split_ref[members:2 * members, lanes] = low

    def pick():
        both = jnp.dot(split_ref[...], hot_ref[...], preferred_element_type=F32)
        return both[:members] + both[members:], both[:members].astype(BF), both[members:].astype(BF)

    def apply(change, high, low):
        c_high, c_low = split(change)
        c_high, c_low = c_high[:, :members], c_low[:, :members]
        both = jnp.dot(jnp.concatenate([c_high, c_low], axis=0), high, preferred_element_type=F32)
        rest = jnp.dot(c_high, low, preferred_element_type=F32)
        return both[:change.shape[0]] + both[change.shape[0]:] + rest

    def own_rows(x):
        own = x[0:members_dev]
        for m in range(1, nm):
            own = jnp.where(ma == m, x[m * members_dev:(m + 1) * members_dev], own)
        filler = jnp.zeros((-members_dev % 16, x.shape[1]), F32)
        return jnp.concatenate([own, filler], axis=0)

    width = 4 if nx % 4 == 0 else nx
    lane = lax.broadcasted_iota(jnp.int32, (members, PAD), 1)
    top_lane = lane[:mid]
    denom = members - 1.0
    prior = pick()[0]
    for sent, received in loc_copies:
        sent.wait_send()
        received.wait_recv()

    change = mixing = None
    for k in range(blocks):
        slot = k % 2
        b = order_ref[k]
        error_var = var_ref[pl.ds(b, 1), :]
        obs_mean = jnp.sum(prior, axis=0, keepdims=True) / members
        anomaly = prior - obs_mean
        variance = jnp.sum(anomaly * anomaly, axis=0, keepdims=True) / denom
        total_var = variance + error_var
        innovation = value_ref[pl.ds(b, 1), :] - obs_mean
        shrink = 1.0 / (1.0 + jnp.sqrt(error_var / total_var))
        scaled = 1.0 / (denom * total_var)
        mean_gain = innovation * scaled
        spread_gain = shrink * scaled
        a_high, a_low = split(anomaly)
        anom_ref[0:members, :] = a_high
        anom_ref[PAD:PAD + members, :] = a_low

        def group(c, turn, g):
            for j in range(width):
                taper = loc_all[(g * width + j) * ny + c, pl.ds(b, 1), :]
                w_high, w_low = split(anomaly * (taper * spread_gain))
                lhs_ref[turn, 2 * j * members:(2 * j + 1) * members, :] = w_high
                lhs_ref[turn, (2 * j + 1) * members:(2 * j + 2) * members, :] = w_low
                gm_ref[turn, j:j + 1, :] = taper * mean_gain
            end = 2 * width * members
            g_high, g_low = split(gm_ref[turn])
            lhs_ref[turn, end:end + 16, :] = jnp.concatenate([g_high, g_low], axis=0)
            product = lax.dot_general(
                lhs_ref[turn], anom_ref[...], (((1,), (1,)), ((), ())), preferred_element_type=F32
            )
            shift = product[end:end + 8, :PAD] + product[end:end + 8, PAD:] + product[end + 8:end + 16, :PAD]
            for j in range(width):
                first = product[2 * j * members:(2 * j + 1) * members]
                second = product[(2 * j + 1) * members:(2 * j + 2) * members, :PAD]
                spread = first[:, :PAD] + first[:, PAD:] + second
                x = g * width + j
                send_ref[slot, c, x, 0:mid, :] = jnp.where(
                    top_lane < members, spread[:mid], pltpu.roll(spread[mid:], mid, 1)
                )
                send_ref[slot, c, x, mid:mid + 8, :] = jnp.broadcast_to(shift[j:j + 1], (8, PAD))

        def contribute(c, turn):
            if nx == width:
                group(c, turn, 0)
            else:
                lax.fori_loop(0, nx // width, lambda g, carry: (group(c, turn, g), carry)[1], 0)

        contribute(other, 0)
        pair = remote(
            send_ref.at[slot, other], pair_ref.at[slot], pair_sem.at[slot, 0], pair_sem.at[slot, 1], (gx, other, ma)
        )
        pair.start()
        contribute(gy, 1)
        pair.wait()
        copies = []
        for d in list(range(1, nx)) + [0]:
            x = lax.rem(gx + d, nx)
            if d == 0:
                line_ref[slot, gx] = send_ref[slot, gy, gx] + pair_ref[slot, gx]
                continue
            send_ref[slot, gy, x] = send_ref[slot, gy, x] + pair_ref[slot, x]
            copy = remote(
                send_ref.at[slot, gy, x], line_ref.at[slot, gx],
                line_send.at[slot, d], line_recv.at[slot, gx], (x, gy, ma),
            )
            copy.start()
            copies.append((copy, remote(
                send_ref.at[slot, gy, x], line_ref.at[slot, x],
                line_send.at[slot, d], line_recv.at[slot, x], (x, gy, ma),
            )))

        if k + 1 < blocks:
            make_hot(k + 1)
            base, high, low = pick()
        else:
            base, high, low = flat_ref[...], split_ref[0:members, :], split_ref[members:2 * members, :]
        if k:
            if k == 1:
                change = mixing
            else:
                change = change + mixing + apply(mixing, *split(change))
            base = base + apply(change, high, low)
            high, low = split(base)
        if k + 1 == blocks:
            base = own_rows(base)

        for sent, received in copies:
            sent.wait_send()
            received.wait_recv()
        total = line_ref[slot, 0]
        for x in range(1, nx):
            total = total + line_ref[slot, x]
        top = total[:mid]
        turned = jnp.concatenate([top, jnp.zeros((PAD - mid, PAD), F32)], axis=0).T
        bottom = jnp.where(top_lane < mid, turned[mid:members], pltpu.roll(top, PAD - mid, 1))
        mixing = total[mid:mid + 1] - jnp.concatenate([top, bottom], axis=0)
        mixing = jnp.where(lane < members, mixing, 0.0)
        centre = jnp.sum(mixing, axis=1, keepdims=True) / members
        mixing = jnp.where(lane < members, mixing - centre, 0.0)
        if k + 1 < blocks:
            prior = base + apply(mixing, high, low)

    mine = base + apply(own_rows(mixing), high, low)
    for lev in range(levels):
        for x in range(cx):
            s = lev * cx + x
            out_ref[:, lev, x, :] = mine[0:members_dev, s * cy:(s + 1) * cy]


def local(
    ensemble, wind_field, obs_value, obs_var, obs_region, obs_cell, block_order, localization
):
    nx, ny, nm = lax.axis_size("gx"), lax.axis_size("gy"), lax.axis_size("ma")
    members_dev, levels, cx, cy = ensemble.shape
    half = members_dev // 2
    members = members_dev * nm
    blocks, obs = obs_value.shape
    rows = levels * cx
    cells = rows * cy
    regions = nx * ny
    width = 4 if nx % 4 == 0 else nx
    dma = pltpu.SemaphoreType.DMA
    vmem = pl.BlockSpec(memory_space=pltpu.VMEM)
    return pl.pallas_call(
        functools.partial(kernel, nx, ny, nm),
        out_shape=jax.ShapeDtypeStruct(ensemble.shape, F32),
        in_specs=[pl.BlockSpec(memory_space=pltpu.SMEM)] + [vmem] * 7,
        out_specs=vmem,
        scratch_shapes=[
            pltpu.VMEM((half, levels, cx, cy), F32),
            pltpu.VMEM(wind_field.shape, F32),
            pltpu.VMEM((ny, half + 2, 2 * levels, cy), F32),
            pltpu.VMEM((ny, half + 2, 2 * levels, cy), F32),
            pltpu.VMEM((ny, half + 2, 2 * levels, cy), F32),
            pltpu.VMEM((ny, half + 2, 2 * levels, cy), F32),
            pltpu.VMEM((half + 2, levels, cx + 4, 2 * cy), F32),
            pltpu.VMEM((ny, half, rows, cy), F32),
            pltpu.VMEM((members, rows, cy), F32),
            pltpu.VMEM((members, cells), F32),
            pltpu.VMEM((2 * members, cells), BF),
            pltpu.VMEM((regions, blocks, obs), F32),
            pltpu.VMEM((cells, obs), BF),
            pltpu.VMEM((2, 2 * width * members + 16, obs), BF),
            pltpu.VMEM((2, 8, obs), F32),
            pltpu.VMEM((2 * PAD, obs), BF),
            pltpu.VMEM((2, ny, nx, members // 2 + 8, PAD), F32),
            pltpu.VMEM((2, nx, members // 2 + 8, PAD), F32),
            pltpu.VMEM((2, nx, members // 2 + 8, PAD), F32),
            dma((4,)),
            dma((2, ny)),
            dma((2, ny)),
            dma((regions,)),
            dma((regions,)),
            dma((nm * ny,)),
            dma((nm * ny,)),
            dma((2, 2)),
            dma((2, nx)),
            dma((2, nx)),
        ],
        compiler_params=pltpu.CompilerParams(
            collective_id=0, has_side_effects=True, vmem_limit_bytes=56 * 1024 * 1024
        ),
    )(block_order, ensemble, wind_field, obs_value, obs_var, obs_region, obs_cell, localization)


def solution(mesh):
    in_specs = (
        P("ma", None, "gx", "gy"),
        P(None, None, "gx", "gy"),
        P(),
        P(),
        P(),
        P(),
        P(),
        P("gx", "gy", None, None),
    )
    out_specs = P("ma", None, "gx", "gy")
    return jax.shard_map(local, mesh=mesh, in_specs=in_specs, out_specs=out_specs, check_vma=False)
```

time: 56.3 us -> 48.3 us (0.86)
  Pallas kernels: 54.6 us -> 46.5 us
    pallas_call x1, Pallas kernels: 54.6 us -> 46.5 us  [local(): pl.pallas_call(functools.partial(kernel, nx, ny, nm), out_shape=jax.Shape...]
where the time goes in v2:
time: 48.3 us; the launch traced here: 48.1 us
  Pallas kernels  46.5 us (96%)
  local copies, waits for them, and re-layouts  1.53 us (3%)
    pallas_call x1, Pallas kernels, local(): pl.pallas_call(functools.partial(kernel, nx, ny, nm), out_shape=jax.Shape...  46.5 us
    unnamed x1, local copies, waits for them, and re-layouts  1.53 us

profile of v2, /device:TPU:0, one launch (start us, length us, event | category | flops | bytes accessed | tf_op | source)
XLA Modules:
  0.0 48.1 jit_solution(3463763778467699167)
XLA Ops:
  0.0 46.5 %shard_map.82 = f32[20,2,4,128]{3,2,1,0:T(4,128)} custom-call(s32[4]{0:T(128)} %order_ref.1, f32[20,2,4,128]{3,2,1,0:T(4,128)} %ens_ref.1, f32[2,2,4,128]{3,2,1,0:T(4,128)} %wind_ref.1, f32[4,1024]{1,0:T(4,128)} %value_ref.1, f32[4,1024]{1,0:T(4,128)} %var_ref.1, s32[4,1024]{1,0:T(4,128)} %region_ref.1, s32[4,1024]{1,0:T(4,128)} %cell_ref.1, ...), custom_call_target="tpu_custom_call" | custom-call | tf_op jit(solution)/shard_map/pallas_call | solution.py:327
  46.5 1.5 %copy.10 = f32[20,2,4,128]{3,2,1,0:T(4,128)} copy(f32[20,2,4,128]{3,2,1,0:T(4,128)} %shard_map.82) | data formatting | bytes 163840

commit v3 on v2

--- a/solution.py
+++ b/solution.py
@@ -25,7 +25,7 @@
     order_ref, ens_ref, wind_ref, value_ref, var_ref, region_ref, cell_ref, loc_ref,
     out_ref,
     o_ens, o_wind, up_ref, down_ref, low_ref, high_ref, ext_ref, piece_ref,
-    all_ref, flat_ref, split_ref, loc_all, hot_ref, lhs_ref, gm_ref, anom_ref,
+    all_ref, flat_ref, split_ref, loc_all, hot_ref, lhs_ref, next_ref, anom_ref,
     send_ref, pair_ref, line_ref,
     swap_sem, halo_send, halo_recv, loc_send, loc_recv, plane_send, plane_recv,
     pair_sem, line_send, line_recv,
@@ -66,7 +66,6 @@
             down_ref[c, 0:half, pair_rows, :] = part[:, 0:2]
             down_ref[c, half:half + 2, pair_rows, :] = winds[:, 0:2]
     anom_ref[...] = jnp.zeros_like(anom_ref)
-    gm_ref[...] = jnp.zeros_like(gm_ref)
 
     pl.semaphore_wait(barrier, len(line) + len(plane) - (ny - 1))
 
@@ -102,9 +101,10 @@
         cell = jnp.where(region_ref[pl.ds(b, 1), :] == own_region, cell_ref[pl.ds(b, 1), :], -1)
         for s in range(cells // PAD):
             index = lax.broadcasted_iota(jnp.int32, (PAD, obs), 0) + s * PAD
-            hot_ref[s * PAD:(s + 1) * PAD, :] = jnp.where(index == cell, 1.0, 0.0).astype(BF)
+            hot_ref[k, s * PAD:(s + 1) * PAD, :] = jnp.where(index == cell, 1.0, 0.0).astype(BF)
 
     make_hot(0)
+    make_hot(1)
     for copy in swap:
         copy.wait()
 
@@ -161,6 +161,8 @@
             plane_send.at[i], plane_recv.at[source], (gx, c, m),
         )))
     all_ref[pl.ds(own_part * half, half)] = piece_ref[gy]
+    for k in range(2, blocks):
+        make_hot(k)
     for sent, received in plane_copies:
         sent.wait_send()
         received.wait_recv()
@@ -173,16 +175,19 @@
         split_ref[0:members, lanes] = high
         split_ref[members:2 * members, lanes] = low
 
-    def pick():
-        both = jnp.dot(split_ref[...], hot_ref[...], preferred_element_type=F32)
+    def pick(k):
+        both = jnp.dot(split_ref[...], hot_ref[k], preferred_element_type=F32)
         return both[:members] + both[members:], both[:members].astype(BF), both[members:].astype(BF)
 
-    def apply(change, high, low):
-        c_high, c_low = split(change)
-        c_high, c_low = c_high[:, :members], c_low[:, :members]
-        both = jnp.dot(jnp.concatenate([c_high, c_low], axis=0), high, preferred_element_type=F32)
-        rest = jnp.dot(c_high, low, preferred_element_type=F32)
-        return both[:change.shape[0]] + both[change.shape[0]:] + rest
+    def stack(high, low):
+        return jnp.concatenate([high, low, high], axis=0)
+
+    def apply(change, stacked):
+        high = change.astype(BF).astype(F32)
+        blank = jnp.zeros_like(change)
+        high, low = (jnp.concatenate([part, blank], axis=1) for part in (high, change - high))
+        wide = high + pltpu.roll(high, members, 1) + pltpu.roll(low, 2 * members, 1)
+        return jnp.dot(wide.astype(BF)[:, :3 * members], stacked, preferred_element_type=F32)
 
     def own_rows(x):
         own = x[0:members_dev]
@@ -195,7 +200,7 @@
     lane = lax.broadcasted_iota(jnp.int32, (members, PAD), 1)
     top_lane = lane[:mid]
     denom = members - 1.0
-    prior = pick()[0]
+    prior = pick(0)[0]
     for sent, received in loc_copies:
         sent.wait_send()
         received.wait_recv()
@@ -212,11 +217,14 @@
         innovation = value_ref[pl.ds(b, 1), :] - obs_mean
         shrink = 1.0 / (1.0 + jnp.sqrt(error_var / total_var))
         scaled = 1.0 / (denom * total_var)
-        mean_gain = innovation * scaled
+        lift = innovation * (1.0 + jnp.sqrt(error_var / total_var))
         spread_gain = shrink * scaled
         a_high, a_low = split(anomaly)
         anom_ref[0:members, :] = a_high
         anom_ref[PAD:PAD + members, :] = a_low
+        lift_high, lift_low = split(jnp.concatenate([lift, jnp.zeros((15, obs), F32)], axis=0))
+        anom_ref[members:members + 16, :] = lift_high
+        anom_ref[PAD + members:PAD + members + 16, :] = lift_low
 
         def group(c, turn, g):
             for j in range(width):
@@ -224,23 +232,17 @@
                 w_high, w_low = split(anomaly * (taper * spread_gain))
                 lhs_ref[turn, 2 * j * members:(2 * j + 1) * members, :] = w_high
                 lhs_ref[turn, (2 * j + 1) * members:(2 * j + 2) * members, :] = w_low
-                gm_ref[turn, j:j + 1, :] = taper * mean_gain
-            end = 2 * width * members
-            g_high, g_low = split(gm_ref[turn])
-            lhs_ref[turn, end:end + 16, :] = jnp.concatenate([g_high, g_low], axis=0)
             product = lax.dot_general(
                 lhs_ref[turn], anom_ref[...], (((1,), (1,)), ((), ())), preferred_element_type=F32
             )
-            shift = product[end:end + 8, :PAD] + product[end:end + 8, PAD:] + product[end + 8:end + 16, :PAD]
             for j in range(width):
                 first = product[2 * j * members:(2 * j + 1) * members]
                 second = product[(2 * j + 1) * members:(2 * j + 2) * members, :PAD]
                 spread = first[:, :PAD] + first[:, PAD:] + second
                 x = g * width + j
-                send_ref[slot, c, x, 0:mid, :] = jnp.where(
-                    top_lane < members, spread[:mid], pltpu.roll(spread[mid:], mid, 1)
-                )
-                send_ref[slot, c, x, mid:mid + 8, :] = jnp.broadcast_to(shift[j:j + 1], (8, PAD))
+                packed = jnp.where(top_lane < members, spread[:mid], pltpu.roll(spread[mid:], mid, 1))
+                last = members + mid + 1
+                send_ref[slot, c, x] = jnp.where(top_lane == last, pltpu.roll(spread[:mid], mid + 1, 1), packed)
 
         def contribute(c, turn):
             if nx == width:
@@ -273,17 +275,17 @@
             )))
 
         if k + 1 < blocks:
-            make_hot(k + 1)
-            base, high, low = pick()
+            base, high, low = pick(k + 1)
         else:
             base, high, low = flat_ref[...], split_ref[0:members, :], split_ref[members:2 * members, :]
         if k:
             if k == 1:
                 change = mixing
             else:
-                change = change + mixing + apply(mixing, *split(change))
-            base = base + apply(change, high, low)
+                change = change + mixing + apply(mixing, stack(*split(change)))
+            base = base + apply(change, stack(high, low))
             high, low = split(base)
+        next_ref[...] = stack(high, low)
         if k + 1 == blocks:
             base = own_rows(base)
 
@@ -293,17 +295,19 @@
         total = line_ref[slot, 0]
         for x in range(1, nx):
             total = total + line_ref[slot, x]
-        top = total[:mid]
+        top = total
         turned = jnp.concatenate([top, jnp.zeros((PAD - mid, PAD), F32)], axis=0).T
         bottom = jnp.where(top_lane < mid, turned[mid:members], pltpu.roll(top, PAD - mid, 1))
-        mixing = total[mid:mid + 1] - jnp.concatenate([top, bottom], axis=0)
+        last = members + mid
+        shift = turned[last + 1:last + 2] + pltpu.roll(turned[last:last + 8], mid, 1)[0:1]
+        mixing = shift - jnp.concatenate([top, bottom], axis=0)
         mixing = jnp.where(lane < members, mixing, 0.0)
         centre = jnp.sum(mixing, axis=1, keepdims=True) / members
         mixing = jnp.where(lane < members, mixing - centre, 0.0)
         if k + 1 < blocks:
-            prior = base + apply(mixing, high, low)
-
-    mine = base + apply(own_rows(mixing), high, low)
+            prior = base + apply(mixing, next_ref[...])
+
+    mine = base + apply(own_rows(mixing), next_ref[...])
     for lev in range(levels):
         for x in range(cx):
             s = lev * cx + x
@@ -342,13 +346,13 @@
             pltpu.VMEM((members, cells), F32),
             pltpu.VMEM((2 * members, cells), BF),
             pltpu.VMEM((regions, blocks, obs), F32),
-            pltpu.VMEM((cells, obs), BF),
-            pltpu.VMEM((2, 2 * width * members + 16, obs), BF),
-            pltpu.VMEM((2, 8, obs), F32),
+            pltpu.VMEM((blocks, cells, obs), BF),
+            pltpu.VMEM((2, 2 * width * members, obs), BF),
+            pltpu.VMEM((3 * members, cells), BF),
             pltpu.VMEM((2 * PAD, obs), BF),
-            pltpu.VMEM((2, ny, nx, members // 2 + 8, PAD), F32),
-            pltpu.VMEM((2, nx, members // 2 + 8, PAD), F32),
-            pltpu.VMEM((2, nx, members // 2 + 8, PAD), F32),
+            pltpu.VMEM((2, ny, nx, members // 2, PAD), F32),
+            pltpu.VMEM((2, nx, members // 2, PAD), F32),
+            pltpu.VMEM((2, nx, members // 2, PAD), F32),
             dma((4,)),
             dma((2, ny)),
             dma((2, ny)),

time: 48.3 us -> 47.6 us (0.986)
  Pallas kernels: 46.5 us -> 45.8 us
    pallas_call x1, Pallas kernels: 46.5 us -> 45.8 us  [local(): pl.pallas_call(functools.partial(kernel, nx, ny, nm), out_shape=jax.Shape...]
where the time goes in v3:
time: 47.6 us; the launch traced here: 47.4 us
  Pallas kernels  45.8 us (96%)
  local copies, waits for them, and re-layouts  1.53 us (3%)
    pallas_call x1, Pallas kernels, local(): pl.pallas_call(functools.partial(kernel, nx, ny, nm), out_shape=jax.Shape...  45.8 us
    unnamed x1, local copies, waits for them, and re-layouts  1.53 us

profile of v3, /device:TPU:0, one launch (start us, length us, event | category | flops | bytes accessed | tf_op | source)
XLA Modules:
  0.0 47.4 jit_solution(6494169255436345882)
XLA Ops:
  0.0 45.8 %shard_map.82 = f32[20,2,4,128]{3,2,1,0:T(4,128)} custom-call(s32[4]{0:T(128)} %order_ref.1, f32[20,2,4,128]{3,2,1,0:T(4,128)} %ens_ref.1, f32[2,2,4,128]{3,2,1,0:T(4,128)} %wind_ref.1, f32[4,1024]{1,0:T(4,128)} %value_ref.1, f32[4,1024]{1,0:T(4,128)} %var_ref.1, s32[4,1024]{1,0:T(4,128)} %region_ref.1, s32[4,1024]{1,0:T(4,128)} %cell_ref.1, ...), custom_call_target="tpu_custom_call" | custom-call | tf_op jit(solution)/shard_map/pallas_call | solution.py:331
  45.9 1.5 %copy.10 = f32[20,2,4,128]{3,2,1,0:T(4,128)} copy(f32[20,2,4,128]{3,2,1,0:T(4,128)} %shard_map.82) | data formatting | bytes 163840

commit v4 on v3

--- a/solution.py
+++ b/solution.py
@@ -22,8 +22,9 @@
 
 def kernel(
     nx, ny, nm,
-    order_ref, ens_ref, wind_ref, value_ref, var_ref, region_ref, cell_ref, loc_ref,
+    order_ref, ens_in, wind_in, value_in, var_in, region_in, cell_in, loc_in,
     out_ref,
+    ens_ref, wind_ref, value_ref, var_ref, region_ref, cell_ref, loc_ref, in_sem,
     o_ens, o_wind, up_ref, down_ref, low_ref, high_ref, ext_ref, piece_ref,
     all_ref, flat_ref, split_ref, loc_all, hot_ref, lhs_ref, next_ref, anom_ref,
     send_ref, pair_ref, line_ref,
@@ -56,6 +57,18 @@
     for m, c in plane[ny - 1:]:
         pl.semaphore_signal(barrier, inc=1, device_id=(gx, c, m), device_id_type=MESH)
 
+    inputs = [
+        pltpu.make_async_copy(src, dst, in_sem.at[i])
+        for i, (src, dst) in enumerate((
+            (ens_in, ens_ref), (wind_in, wind_ref), (region_in, region_ref), (cell_in, cell_ref),
+            (loc_in, loc_ref), (value_in, value_ref), (var_in, var_ref),
+        ))
+    ]
+    for copy in inputs:
+        copy.start()
+    for copy in inputs[:2]:
+        copy.wait()
+
     for c in range(ny):
         for lev in range(levels):
             pair_rows = slice(2 * lev, 2 * lev + 2)
@@ -67,6 +80,8 @@
             down_ref[c, half:half + 2, pair_rows, :] = winds[:, 0:2]
     anom_ref[...] = jnp.zeros_like(anom_ref)
 
+    for copy in inputs[2:]:
+        copy.wait()
     pl.semaphore_wait(barrier, len(line) + len(plane) - (ny - 1))
 
     after, before = lax.rem(gx + 1, nx), lax.rem(gx + nx - 1, nx)
@@ -196,7 +211,6 @@
         filler = jnp.zeros((-members_dev % 16, x.shape[1]), F32)
         return jnp.concatenate([own, filler], axis=0)
 
-    width = 4 if nx % 4 == 0 else nx
     lane = lax.broadcasted_iota(jnp.int32, (members, PAD), 1)
     top_lane = lane[:mid]
     denom = members - 1.0
@@ -226,53 +240,61 @@
         anom_ref[members:members + 16, :] = lift_high
         anom_ref[PAD + members:PAD + members + 16, :] = lift_low
 
-        def group(c, turn, g):
-            for j in range(width):
-                taper = loc_all[(g * width + j) * ny + c, pl.ds(b, 1), :]
+        def pair_copy(x):
+            return remote(
+                send_ref.at[slot, other, x], pair_ref.at[slot, x],
+                pair_sem.at[slot, 0, x], pair_sem.at[slot, 1, x], (gx, other, ma),
+            )
+
+        def line_copy(x, place):
+            return remote(
+                send_ref.at[slot, gy, x], line_ref.at[slot, place],
+                line_send.at[slot, x], line_recv.at[slot, place], (x, gy, ma),
+            )
+
+        def terms(x, turn):
+            for c in range(ny):
+                taper = loc_all[x * ny + c, pl.ds(b, 1), :]
                 w_high, w_low = split(anomaly * (taper * spread_gain))
-                lhs_ref[turn, 2 * j * members:(2 * j + 1) * members, :] = w_high
-                lhs_ref[turn, (2 * j + 1) * members:(2 * j + 2) * members, :] = w_low
+                lhs_ref[turn, 2 * c * members:(2 * c + 1) * members, :] = w_high
+                lhs_ref[turn, (2 * c + 1) * members:(2 * c + 2) * members, :] = w_low
             product = lax.dot_general(
                 lhs_ref[turn], anom_ref[...], (((1,), (1,)), ((), ())), preferred_element_type=F32
             )
-            for j in range(width):
-                first = product[2 * j * members:(2 * j + 1) * members]
-                second = product[(2 * j + 1) * members:(2 * j + 2) * members, :PAD]
+            for c in range(ny):
+                first = product[2 * c * members:(2 * c + 1) * members]
+                second = product[(2 * c + 1) * members:(2 * c + 2) * members, :PAD]
                 spread = first[:, :PAD] + first[:, PAD:] + second
-                x = g * width + j
                 packed = jnp.where(top_lane < members, spread[:mid], pltpu.roll(spread[mid:], mid, 1))
                 last = members + mid + 1
                 send_ref[slot, c, x] = jnp.where(top_lane == last, pltpu.roll(spread[:mid], mid + 1, 1), packed)
-
-        def contribute(c, turn):
-            if nx == width:
-                group(c, turn, 0)
+            pair_copy(x).start()
+
+        def forward(x, away):
+            pair_copy(x).wait()
+            both = send_ref[slot, gy, x] + pair_ref[slot, x]
+            if away:
+                send_ref[slot, gy, x] = both
+                line_copy(x, gx).start()
             else:
-                lax.fori_loop(0, nx // width, lambda g, carry: (group(c, turn, g), carry)[1], 0)
-
-        contribute(other, 0)
-        pair = remote(
-            send_ref.at[slot, other], pair_ref.at[slot], pair_sem.at[slot, 0], pair_sem.at[slot, 1], (gx, other, ma)
-        )
-        pair.start()
-        contribute(gy, 1)
-        pair.wait()
-        copies = []
-        for d in list(range(1, nx)) + [0]:
-            x = lax.rem(gx + d, nx)
-            if d == 0:
-                line_ref[slot, gx] = send_ref[slot, gy, gx] + pair_ref[slot, gx]
-                continue
-            send_ref[slot, gy, x] = send_ref[slot, gy, x] + pair_ref[slot, x]
-            copy = remote(
-                send_ref.at[slot, gy, x], line_ref.at[slot, gx],
-                line_send.at[slot, d], line_recv.at[slot, gx], (x, gy, ma),
-            )
-            copy.start()
-            copies.append((copy, remote(
-                send_ref.at[slot, gy, x], line_ref.at[slot, x],
-                line_send.at[slot, d], line_recv.at[slot, x], (x, gy, ma),
-            )))
+                line_ref[slot, x] = both
+
+        ahead = [lax.rem(gx + d, nx) for d in range(nx)]
+        if nx <= 8:
+            order = ahead[2:3] + ahead[1:2] + ahead[3:] + ahead[:1]
+            for i, x in enumerate(order):
+                terms(x, i % 2)
+                if i:
+                    forward(order[i - 1], True)
+        else:
+            def step(d, carry):
+                terms(lax.rem(gx + d, nx), 0)
+                forward(lax.rem(gx + d, nx), True)
+                return carry
+
+            lax.fori_loop(1, nx, step, 0)
+            terms(gx, 1)
+        forward(gx, False)
 
         if k + 1 < blocks:
             base, high, low = pick(k + 1)
@@ -289,9 +311,9 @@
         if k + 1 == blocks:
             base = own_rows(base)
 
-        for sent, received in copies:
-            sent.wait_send()
-            received.wait_recv()
+        for x in ahead[1:]:
+            line_copy(x, gx).wait_send()
+            line_copy(x, x).wait_recv()
         total = line_ref[slot, 0]
         for x in range(1, nx):
             total = total + line_ref[slot, x]
@@ -325,15 +347,22 @@
     rows = levels * cx
     cells = rows * cy
     regions = nx * ny
-    width = 4 if nx % 4 == 0 else nx
     dma = pltpu.SemaphoreType.DMA
     vmem = pl.BlockSpec(memory_space=pltpu.VMEM)
     return pl.pallas_call(
         functools.partial(kernel, nx, ny, nm),
         out_shape=jax.ShapeDtypeStruct(ensemble.shape, F32),
-        in_specs=[pl.BlockSpec(memory_space=pltpu.SMEM)] + [vmem] * 7,
+        in_specs=[pl.BlockSpec(memory_space=pltpu.SMEM)] + [pl.BlockSpec(memory_space=pl.ANY)] * 7,
         out_specs=vmem,
         scratch_shapes=[
+            pltpu.VMEM(ensemble.shape, F32),
+            pltpu.VMEM(wind_field.shape, F32),
+            pltpu.VMEM(obs_value.shape, F32),
+            pltpu.VMEM(obs_var.shape, F32),
+            pltpu.VMEM(obs_region.shape, jnp.int32),
+            pltpu.VMEM(obs_cell.shape, jnp.int32),
+            pltpu.VMEM(localization.shape, F32),
+            dma((7,)),
             pltpu.VMEM((half, levels, cx, cy), F32),
             pltpu.VMEM(wind_field.shape, F32),
             pltpu.VMEM((ny, half + 2, 2 * levels, cy), F32),
@@ -347,7 +376,7 @@
             pltpu.VMEM((2 * members, cells), BF),
             pltpu.VMEM((regions, blocks, obs), F32),
             pltpu.VMEM((blocks, cells, obs), BF),
-            pltpu.VMEM((2, 2 * width * members, obs), BF),
+            pltpu.VMEM((2, 2 * ny * members, obs), BF),
             pltpu.VMEM((3 * members, cells), BF),
             pltpu.VMEM((2 * PAD, obs), BF),
             pltpu.VMEM((2, ny, nx, members // 2, PAD), F32),
@@ -360,7 +389,7 @@
             dma((regions,)),
             dma((nm * ny,)),
             dma((nm * ny,)),
-            dma((2, 2)),
+            dma((2, 2, nx)),
             dma((2, nx)),
             dma((2, nx)),
         ],

time: 47.6 us -> 48.3 us (1.015)
  Pallas kernels: 45.8 us -> 46.6 us
    pallas_call x1, Pallas kernels: 45.8 us -> 46.6 us  [local(): pl.pallas_call(functools.partial(kernel, nx, ny, nm), out_shape=jax.Shape...]
where the time goes in v4:
time: 48.3 us; the launch traced here: 48.1 us
  Pallas kernels  46.6 us (96%)
  local copies, waits for them, and re-layouts  1.53 us (3%)
    pallas_call x1, Pallas kernels, local(): pl.pallas_call(functools.partial(kernel, nx, ny, nm), out_shape=jax.Shape...  46.6 us
    unnamed x1, local copies, waits for them, and re-layouts  1.53 us

profile of v4, /device:TPU:0, one launch (start us, length us, event | category | flops | bytes accessed | tf_op | source)
XLA Modules:
  0.0 48.1 jit_solution(14704030247234881170)
XLA Ops:
  0.0 46.6 %shard_map.82 = f32[20,2,4,128]{3,2,1,0:T(4,128)} custom-call(s32[4]{0:T(128)} %order_ref.1, f32[20,2,4,128]{3,2,1,0:T(4,128)} %ens_in.1, f32[2,2,4,128]{3,2,1,0:T(4,128)} %wind_in.1, f32[4,1024]{1,0:T(4,128)} %value_in.1, f32[4,1024]{1,0:T(4,128)} %var_in.1, s32[4,1024]{1,0:T(4,128)} %region_in.1, s32[4,1024]{1,0:T(4,128)} %cell_in.1, f32[1,1,4,1024]{3,2,1,0:T(4,128)} %loc_in.1), custom_call_target="tpu_custom_call" | custom-call | tf_op jit(solution)/shard_map/pallas_call | solution.py:352
  46.6 1.5 %copy.10 = f32[20,2,4,128]{3,2,1,0:T(4,128)} copy(f32[20,2,4,128]{3,2,1,0:T(4,128)} %shard_map.82) | data formatting | bytes 163840

commit v5 on v3

--- a/solution.py
+++ b/solution.py
@@ -22,11 +22,12 @@
 
 def kernel(
     nx, ny, nm,
-    order_ref, ens_ref, wind_ref, value_ref, var_ref, region_ref, cell_ref, loc_ref,
+    order_ref, ens_in, wind_in, value_in, var_in, region_in, cell_in, loc_in,
     out_ref,
+    ens_ref, wind_ref, value_ref, var_ref, region_ref, cell_ref, loc_ref, in_sem,
     o_ens, o_wind, up_ref, down_ref, low_ref, high_ref, ext_ref, piece_ref,
     all_ref, flat_ref, split_ref, loc_all, hot_ref, lhs_ref, next_ref, anom_ref,
-    send_ref, pair_ref, line_ref,
+    send_ref, pair_ref, line_ref, base_ref, part_ref, prior_ref, mixing_ref, change_ref,
     swap_sem, halo_send, halo_recv, loc_send, loc_recv, plane_send, plane_recv,
     pair_sem, line_send, line_recv,
 ):
@@ -56,6 +57,18 @@
     for m, c in plane[ny - 1:]:
         pl.semaphore_signal(barrier, inc=1, device_id=(gx, c, m), device_id_type=MESH)
 
+    inputs = [
+        pltpu.make_async_copy(src, dst, in_sem.at[i])
+        for i, (src, dst) in enumerate((
+            (ens_in, ens_ref), (wind_in, wind_ref), (region_in, region_ref), (cell_in, cell_ref),
+            (loc_in, loc_ref), (value_in, value_ref), (var_in, var_ref),
+        ))
+    ]
+    for copy in inputs:
+        copy.start()
+    for copy in inputs[:2]:
+        copy.wait()
+
     for c in range(ny):
         for lev in range(levels):
             pair_rows = slice(2 * lev, 2 * lev + 2)
@@ -67,6 +80,8 @@
             down_ref[c, half:half + 2, pair_rows, :] = winds[:, 0:2]
     anom_ref[...] = jnp.zeros_like(anom_ref)
 
+    for copy in inputs[2:]:
+        copy.wait()
     pl.semaphore_wait(barrier, len(line) + len(plane) - (ny - 1))
 
     after, before = lax.rem(gx + 1, nx), lax.rem(gx + nx - 1, nx)
@@ -96,15 +111,15 @@
         loc_copies.append((copy, remote(loc_ref.at[0, 0], loc_all.at[source], loc_send.at[i], loc_recv.at[source], (x, c, ma))))
     loc_all[own_region] = loc_ref[0, 0]
 
-    def make_hot(k):
+    def make_hot(k, carry):
         b = order_ref[k]
         cell = jnp.where(region_ref[pl.ds(b, 1), :] == own_region, cell_ref[pl.ds(b, 1), :], -1)
         for s in range(cells // PAD):
             index = lax.broadcasted_iota(jnp.int32, (PAD, obs), 0) + s * PAD
             hot_ref[k, s * PAD:(s + 1) * PAD, :] = jnp.where(index == cell, 1.0, 0.0).astype(BF)
-
-    make_hot(0)
-    make_hot(1)
+        return carry
+
+    lax.fori_loop(0, 2, make_hot, 0)
     for copy in swap:
         copy.wait()
 
@@ -161,8 +176,7 @@
             plane_send.at[i], plane_recv.at[source], (gx, c, m),
         )))
     all_ref[pl.ds(own_part * half, half)] = piece_ref[gy]
-    for k in range(2, blocks):
-        make_hot(k)
+    lax.fori_loop(2, blocks, make_hot, 0)
     for sent, received in plane_copies:
         sent.wait_send()
         received.wait_recv()
@@ -177,7 +191,8 @@
 
     def pick(k):
         both = jnp.dot(split_ref[...], hot_ref[k], preferred_element_type=F32)
-        return both[:members] + both[members:], both[:members].astype(BF), both[members:].astype(BF)
+        base_ref[...] = both[:members] + both[members:]
+        part_ref[...] = both.astype(BF)
 
     def stack(high, low):
         return jnp.concatenate([high, low, high], axis=0)
@@ -200,15 +215,19 @@
     lane = lax.broadcasted_iota(jnp.int32, (members, PAD), 1)
     top_lane = lane[:mid]
     denom = members - 1.0
-    prior = pick(0)[0]
+    pick(0)
+    prior_ref[...] = base_ref[...]
     for sent, received in loc_copies:
         sent.wait_send()
         received.wait_recv()
 
-    change = mixing = None
-    for k in range(blocks):
-        slot = k % 2
+    mixing_ref[...] = jnp.zeros_like(mixing_ref)
+    change_ref[...] = jnp.zeros_like(change_ref)
+
+    def assimilate(k, carry):
+        slot = lax.rem(k, 2)
         b = order_ref[k]
+        prior = prior_ref[...]
         error_var = var_ref[pl.ds(b, 1), :]
         obs_mean = jnp.sum(prior, axis=0, keepdims=True) / members
         anomaly = prior - obs_mean
@@ -226,6 +245,12 @@
         anom_ref[members:members + 16, :] = lift_high
         anom_ref[PAD + members:PAD + members + 16, :] = lift_low
 
+        def line_copy(x, place):
+            return remote(
+                send_ref.at[slot, gy, x], line_ref.at[slot, place],
+                line_send.at[slot, x], line_recv.at[slot, place], (x, gy, ma),
+            )
+
         def group(c, turn, g):
             for j in range(width):
                 taper = loc_all[(g * width + j) * ny + c, pl.ds(b, 1), :]
@@ -239,10 +264,11 @@
                 first = product[2 * j * members:(2 * j + 1) * members]
                 second = product[(2 * j + 1) * members:(2 * j + 2) * members, :PAD]
                 spread = first[:, :PAD] + first[:, PAD:] + second
-                x = g * width + j
                 packed = jnp.where(top_lane < members, spread[:mid], pltpu.roll(spread[mid:], mid, 1))
                 last = members + mid + 1
-                send_ref[slot, c, x] = jnp.where(top_lane == last, pltpu.roll(spread[:mid], mid + 1, 1), packed)
+                send_ref[slot, c, g * width + j] = jnp.where(
+                    top_lane == last, pltpu.roll(spread[:mid], mid + 1, 1), packed
+                )
 
         def contribute(c, turn):
             if nx == width:
@@ -257,45 +283,34 @@
         pair.start()
         contribute(gy, 1)
         pair.wait()
-        copies = []
-        for d in list(range(1, nx)) + [0]:
-            x = lax.rem(gx + d, nx)
-            if d == 0:
-                line_ref[slot, gx] = send_ref[slot, gy, gx] + pair_ref[slot, gx]
-                continue
+        ahead = [lax.rem(gx + d, nx) for d in range(nx)]
+        for x in ahead[1:]:
             send_ref[slot, gy, x] = send_ref[slot, gy, x] + pair_ref[slot, x]
-            copy = remote(
-                send_ref.at[slot, gy, x], line_ref.at[slot, gx],
-                line_send.at[slot, d], line_recv.at[slot, gx], (x, gy, ma),
-            )
-            copy.start()
-            copies.append((copy, remote(
-                send_ref.at[slot, gy, x], line_ref.at[slot, x],
-                line_send.at[slot, d], line_recv.at[slot, x], (x, gy, ma),
-            )))
-
-        if k + 1 < blocks:
-            base, high, low = pick(k + 1)
-        else:
-            base, high, low = flat_ref[...], split_ref[0:members, :], split_ref[members:2 * members, :]
-        if k:
-            if k == 1:
-                change = mixing
-            else:
-                change = change + mixing + apply(mixing, stack(*split(change)))
-            base = base + apply(change, stack(high, low))
-            high, low = split(base)
-        next_ref[...] = stack(high, low)
-        if k + 1 == blocks:
-            base = own_rows(base)
-
-        for sent, received in copies:
-            sent.wait_send()
-            received.wait_recv()
-        total = line_ref[slot, 0]
+            line_copy(x, gx).start()
+        line_ref[slot, gx] = send_ref[slot, gy, gx] + pair_ref[slot, gx]
+
+        @pl.when(k + 1 < blocks)
+        def _():
+            pick(k + 1)
+
+        @pl.when(k + 1 == blocks)
+        def _():
+            base_ref[...] = flat_ref[...]
+            part_ref[...] = split_ref[...]
+
+        mixing, change = mixing_ref[...], change_ref[...]
+        change = change + mixing + apply(mixing, stack(*split(change)))
+        change_ref[...] = change
+        base = base_ref[...] + apply(change, stack(part_ref[0:members, :], part_ref[members:2 * members, :]))
+        base_ref[...] = base
+        next_ref[...] = stack(*split(base))
+
+        for x in ahead[1:]:
+            line_copy(x, gx).wait_send()
+            line_copy(x, x).wait_recv()
+        top = line_ref[slot, 0]
         for x in range(1, nx):
-            total = total + line_ref[slot, x]
-        top = total
+            top = top + line_ref[slot, x]
         turned = jnp.concatenate([top, jnp.zeros((PAD - mid, PAD), F32)], axis=0).T
         bottom = jnp.where(top_lane < mid, turned[mid:members], pltpu.roll(top, PAD - mid, 1))
         last = members + mid
@@ -304,9 +319,16 @@
         mixing = jnp.where(lane < members, mixing, 0.0)
         centre = jnp.sum(mixing, axis=1, keepdims=True) / members
         mixing = jnp.where(lane < members, mixing - centre, 0.0)
-        if k + 1 < blocks:
-            prior = base + apply(mixing, next_ref[...])
-
+        mixing_ref[...] = mixing
+
+        @pl.when(k + 1 < blocks)
+        def _():
+            prior_ref[...] = base + apply(mixing, next_ref[...])
+
+        return carry
+
+    lax.fori_loop(0, blocks, assimilate, 0)
+    base, mixing = own_rows(base_ref[...]), mixing_ref[...]
     mine = base + apply(own_rows(mixing), next_ref[...])
     for lev in range(levels):
         for x in range(cx):
@@ -331,9 +353,17 @@
     return pl.pallas_call(
         functools.partial(kernel, nx, ny, nm),
         out_shape=jax.ShapeDtypeStruct(ensemble.shape, F32),
-        in_specs=[pl.BlockSpec(memory_space=pltpu.SMEM)] + [vmem] * 7,
+        in_specs=[pl.BlockSpec(memory_space=pltpu.SMEM)] + [pl.BlockSpec(memory_space=pl.ANY)] * 7,
         out_specs=vmem,
         scratch_shapes=[
+            pltpu.VMEM(ensemble.shape, F32),
+            pltpu.VMEM(wind_field.shape, F32),
+            pltpu.VMEM(obs_value.shape, F32),
+            pltpu.VMEM(obs_var.shape, F32),
+            pltpu.VMEM(obs_region.shape, jnp.int32),
+            pltpu.VMEM(obs_cell.shape, jnp.int32),
+            pltpu.VMEM(localization.shape, F32),
+            dma((7,)),
             pltpu.VMEM((half, levels, cx, cy), F32),
             pltpu.VMEM(wind_field.shape, F32),
             pltpu.VMEM((ny, half + 2, 2 * levels, cy), F32),
@@ -353,6 +383,11 @@
             pltpu.VMEM((2, ny, nx, members // 2, PAD), F32),
             pltpu.VMEM((2, nx, members // 2, PAD), F32),
             pltpu.VMEM((2, nx, members // 2, PAD), F32),
+            pltpu.VMEM((members, obs), F32),
+            pltpu.VMEM((2 * members, obs), BF),
+            pltpu.VMEM((members, obs), F32),
+            pltpu.VMEM((members, PAD), F32),
+            pltpu.VMEM((members, PAD), F32),
             dma((4,)),
             dma((2, ny)),
             dma((2, ny)),

time: 47.6 us -> 47.4 us (level)
  no operation moved by 1% of the time
where the time goes in v5:
time: 47.4 us; the launch traced here: 47.2 us
  Pallas kernels  45.7 us (96%)
  local copies, waits for them, and re-layouts  1.53 us (3%)
    pallas_call x1, Pallas kernels, local(): pl.pallas_call(functools.partial(kernel, nx, ny, nm), out_shape=jax.Shape...  45.7 us
    unnamed x1, local copies, waits for them, and re-layouts  1.53 us

profile of v5, /device:TPU:0, one launch (start us, length us, event | category | flops | bytes accessed | tf_op | source)
XLA Modules:
  0.0 47.2 jit_solution(5740941445979643037)
XLA Ops:
  0.0 45.7 %shard_map.82 = f32[20,2,4,128]{3,2,1,0:T(4,128)} custom-call(s32[4]{0:T(128)} %order_ref.1, f32[20,2,4,128]{3,2,1,0:T(4,128)} %ens_in.1, f32[2,2,4,128]{3,2,1,0:T(4,128)} %wind_in.1, f32[4,1024]{1,0:T(4,128)} %value_in.1, f32[4,1024]{1,0:T(4,128)} %var_in.1, s32[4,1024]{1,0:T(4,128)} %region_in.1, s32[4,1024]{1,0:T(4,128)} %cell_in.1, f32[1,1,4,1024]{3,2,1,0:T(4,128)} %loc_in.1), custom_call_target="tpu_custom_call" | custom-call | tf_op jit(solution)/shard_map/pallas_call | solution.py:353
  45.7 1.5 %copy.10 = f32[20,2,4,128]{3,2,1,0:T(4,128)} copy(f32[20,2,4,128]{3,2,1,0:T(4,128)} %shard_map.82) | data formatting | bytes 163840

commit v6 on v5

--- a/solution.py
+++ b/solution.py
@@ -26,7 +26,7 @@
     out_ref,
     ens_ref, wind_ref, value_ref, var_ref, region_ref, cell_ref, loc_ref, in_sem,
     o_ens, o_wind, up_ref, down_ref, low_ref, high_ref, ext_ref, piece_ref,
-    all_ref, flat_ref, split_ref, loc_all, hot_ref, lhs_ref, next_ref, anom_ref,
+    all_ref, flat_ref, split_ref, loc_all, hot_ref, quarter_ref, lhs_ref, next_ref, anom_ref,
     send_ref, pair_ref, line_ref, base_ref, part_ref, prior_ref, mixing_ref, change_ref,
     swap_sem, halo_send, halo_recv, loc_send, loc_recv, plane_send, plane_recv,
     pair_sem, line_send, line_recv,
@@ -38,6 +38,7 @@
     blocks, obs = value_ref.shape
     cells = levels * cx * cy
     rows = levels * cx
+    quarters = cells // (2 * PAD)
     gx, gy, ma = lax.axis_index("gx"), lax.axis_index("gy"), lax.axis_index("ma")
     other = 1 - gy
 
@@ -114,9 +115,12 @@
     def make_hot(k, carry):
         b = order_ref[k]
         cell = jnp.where(region_ref[pl.ds(b, 1), :] == own_region, cell_ref[pl.ds(b, 1), :], -1)
-        for s in range(cells // PAD):
+        quarter = lax.shift_right_arithmetic(cell, 8)
+        quarter_ref[k] = quarter
+        place = jnp.where(cell < 0, -1, cell - quarter * (2 * PAD))
+        for s in range(2):
             index = lax.broadcasted_iota(jnp.int32, (PAD, obs), 0) + s * PAD
-            hot_ref[k, s * PAD:(s + 1) * PAD, :] = jnp.where(index == cell, 1.0, 0.0).astype(BF)
+            hot_ref[k, s * PAD:(s + 1) * PAD, :] = jnp.where(index == place, 1.0, 0.0).astype(BF)
         return carry
 
     lax.fori_loop(0, 2, make_hot, 0)
@@ -186,11 +190,17 @@
         values = all_ref[:, s, :]
         flat_ref[:, lanes] = values
         high, low = split(values)
-        split_ref[0:members, lanes] = high
-        split_ref[members:2 * members, lanes] = low
+        within = slice(s % 2 * cy, (s % 2 + 1) * cy)
+        split_ref[s // 2, 0:members, within] = high
+        split_ref[s // 2, members:2 * members, within] = low
 
     def pick(k):
-        both = jnp.dot(split_ref[...], hot_ref[k], preferred_element_type=F32)
+        quarter = quarter_ref[k]
+        lhs = split_ref[...].reshape(quarters * 2 * members, 2 * PAD)
+        product = jnp.dot(lhs, hot_ref[k], preferred_element_type=F32)
+        both = product[:2 * members]
+        for q in range(1, quarters):
+            both = jnp.where(quarter == q, product[2 * q * members:2 * (q + 1) * members], both)
         base_ref[...] = both[:members] + both[members:]
         part_ref[...] = both.astype(BF)
 
@@ -220,9 +230,6 @@
     for sent, received in loc_copies:
         sent.wait_send()
         received.wait_recv()
-
-    mixing_ref[...] = jnp.zeros_like(mixing_ref)
-    change_ref[...] = jnp.zeros_like(change_ref)
 
     def assimilate(k, carry):
         slot = lax.rem(k, 2)
@@ -296,14 +303,28 @@
         @pl.when(k + 1 == blocks)
         def _():
             base_ref[...] = flat_ref[...]
-            part_ref[...] = split_ref[...]
-
-        mixing, change = mixing_ref[...], change_ref[...]
-        change = change + mixing + apply(mixing, stack(*split(change)))
-        change_ref[...] = change
-        base = base_ref[...] + apply(change, stack(part_ref[0:members, :], part_ref[members:2 * members, :]))
-        base_ref[...] = base
-        next_ref[...] = stack(*split(base))
+            for q in range(quarters):
+                part_ref[:, 2 * q * PAD:2 * (q + 1) * PAD] = split_ref[q]
+
+        @pl.when(k == 1)
+        def _():
+            change_ref[...] = mixing_ref[...]
+
+        @pl.when(k > 1)
+        def _():
+            mixing, change = mixing_ref[...], change_ref[...]
+            change_ref[...] = change + mixing + apply(mixing, stack(*split(change)))
+
+        @pl.when(k > 0)
+        def _():
+            stacked = stack(part_ref[0:members, :], part_ref[members:2 * members, :])
+            base = base_ref[...] + apply(change_ref[...], stacked)
+            base_ref[...] = base
+            high, low = split(base)
+            part_ref[0:members, :] = high
+            part_ref[members:2 * members, :] = low
+
+        next_ref[...] = stack(part_ref[0:members, :], part_ref[members:2 * members, :])
 
         for x in ahead[1:]:
             line_copy(x, gx).wait_send()
@@ -323,7 +344,7 @@
 
         @pl.when(k + 1 < blocks)
         def _():
-            prior_ref[...] = base + apply(mixing, next_ref[...])
+            prior_ref[...] = base_ref[...] + apply(mixing, next_ref[...])
 
         return carry
 
@@ -374,9 +395,10 @@
             pltpu.VMEM((ny, half, rows, cy), F32),
             pltpu.VMEM((members, rows, cy), F32),
             pltpu.VMEM((members, cells), F32),
-            pltpu.VMEM((2 * members, cells), BF),
+            pltpu.VMEM((cells // (2 * PAD), 2 * members, 2 * PAD), BF),
             pltpu.VMEM((regions, blocks, obs), F32),
-            pltpu.VMEM((blocks, cells, obs), BF),
+            pltpu.VMEM((blocks, 2 * PAD, obs), BF),
+            pltpu.VMEM((blocks, 1, obs), jnp.int32),
             pltpu.VMEM((2, 2 * width * members, obs), BF),
             pltpu.VMEM((3 * members, cells), BF),
             pltpu.VMEM((2 * PAD, obs), BF),

time: 47.4 us -> 47.4 us (level)
  no operation moved by 1% of the time
where the time goes in v6:
time: 47.4 us; the launch traced here: 47.2 us
  Pallas kernels  45.6 us (96%)
  local copies, waits for them, and re-layouts  1.53 us (3%)
    pallas_call x1, Pallas kernels, local(): pl.pallas_call(functools.partial(kernel, nx, ny, nm), out_shape=jax.Shape...  45.6 us
    unnamed x1, local copies, waits for them, and re-layouts  1.53 us

profile of v6, /device:TPU:0, one launch (start us, length us, event | category | flops | bytes accessed | tf_op | source)
XLA Modules:
  0.0 47.2 jit_solution(15239694269163825108)
XLA Ops:
  0.0 45.6 %shard_map.82 = f32[20,2,4,128]{3,2,1,0:T(4,128)} custom-call(s32[4]{0:T(128)} %order_ref.1, f32[20,2,4,128]{3,2,1,0:T(4,128)} %ens_in.1, f32[2,2,4,128]{3,2,1,0:T(4,128)} %wind_in.1, f32[4,1024]{1,0:T(4,128)} %value_in.1, f32[4,1024]{1,0:T(4,128)} %var_in.1, s32[4,1024]{1,0:T(4,128)} %region_in.1, s32[4,1024]{1,0:T(4,128)} %cell_in.1, f32[1,1,4,1024]{3,2,1,0:T(4,128)} %loc_in.1), custom_call_target="tpu_custom_call" | custom-call | tf_op jit(solution)/shard_map/pallas_call | solution.py:374
  45.6 1.5 %copy.10 = f32[20,2,4,128]{3,2,1,0:T(4,128)} copy(f32[20,2,4,128]{3,2,1,0:T(4,128)} %shard_map.82) | data formatting | bytes 163840

commit v7 on v6

--- a/solution.py
+++ b/solution.py
@@ -26,7 +26,7 @@
     out_ref,
     ens_ref, wind_ref, value_ref, var_ref, region_ref, cell_ref, loc_ref, in_sem,
     o_ens, o_wind, up_ref, down_ref, low_ref, high_ref, ext_ref, piece_ref,
-    all_ref, flat_ref, split_ref, loc_all, hot_ref, quarter_ref, lhs_ref, next_ref, anom_ref,
+    all_ref, flat_ref, split_ref, loc_all, hot_ref, quarter_ref, lhs_ref, next_ref, anom_ref, turned_ref,
     send_ref, pair_ref, line_ref, base_ref, part_ref, prior_ref, mixing_ref, change_ref,
     swap_sem, halo_send, halo_recv, loc_send, loc_recv, plane_send, plane_recv,
     pair_sem, line_send, line_recv,
@@ -252,6 +252,8 @@
         anom_ref[members:members + 16, :] = lift_high
         anom_ref[PAD + members:PAD + members + 16, :] = lift_low
 
+        turned_ref[...] = anom_ref[...].T
+
         def line_copy(x, place):
             return remote(
                 send_ref.at[slot, gy, x], line_ref.at[slot, place],
@@ -264,9 +266,7 @@
                 w_high, w_low = split(anomaly * (taper * spread_gain))
                 lhs_ref[turn, 2 * j * members:(2 * j + 1) * members, :] = w_high
                 lhs_ref[turn, (2 * j + 1) * members:(2 * j + 2) * members, :] = w_low
-            product = lax.dot_general(
-                lhs_ref[turn], anom_ref[...], (((1,), (1,)), ((), ())), preferred_element_type=F32
-            )
+            product = jnp.dot(lhs_ref[turn], turned_ref[...], preferred_element_type=F32)
             for j in range(width):
                 first = product[2 * j * members:(2 * j + 1) * members]
                 second = product[(2 * j + 1) * members:(2 * j + 2) * members, :PAD]
@@ -402,6 +402,7 @@
             pltpu.VMEM((2, 2 * width * members, obs), BF),
             pltpu.VMEM((3 * members, cells), BF),
             pltpu.VMEM((2 * PAD, obs), BF),
+            pltpu.VMEM((obs, 2 * PAD), BF),
             pltpu.VMEM((2, ny, nx, members // 2, PAD), F32),
             pltpu.VMEM((2, nx, members // 2, PAD), F32),
             pltpu.VMEM((2, nx, members // 2, PAD), F32),

time: 47.4 us -> 47.6 us (level)
  no operation moved by 1% of the time
where the time goes in v7:
time: 47.6 us; the launch traced here: 47.4 us
  Pallas kernels  45.8 us (96%)
  local copies, waits for them, and re-layouts  1.53 us (3%)
    pallas_call x1, Pallas kernels, local(): pl.pallas_call(functools.partial(kernel, nx, ny, nm), out_shape=jax.Shape...  45.8 us
    unnamed x1, local copies, waits for them, and re-layouts  1.53 us

profile of v7, /device:TPU:0, one launch (start us, length us, event | category | flops | bytes accessed | tf_op | source)
XLA Modules:
  0.0 47.4 jit_solution(283072595484137115)
XLA Ops:
  0.0 45.8 %shard_map.82 = f32[20,2,4,128]{3,2,1,0:T(4,128)} custom-call(s32[4]{0:T(128)} %order_ref.1, f32[20,2,4,128]{3,2,1,0:T(4,128)} %ens_in.1, f32[2,2,4,128]{3,2,1,0:T(4,128)} %wind_in.1, f32[4,1024]{1,0:T(4,128)} %value_in.1, f32[4,1024]{1,0:T(4,128)} %var_in.1, s32[4,1024]{1,0:T(4,128)} %region_in.1, s32[4,1024]{1,0:T(4,128)} %cell_in.1, f32[1,1,4,1024]{3,2,1,0:T(4,128)} %loc_in.1), custom_call_target="tpu_custom_call" | custom-call | tf_op jit(solution)/shard_map/pallas_call | solution.py:374
  45.8 1.5 %copy.10 = f32[20,2,4,128]{3,2,1,0:T(4,128)} copy(f32[20,2,4,128]{3,2,1,0:T(4,128)} %shard_map.82) | data formatting | bytes 163840
